TPU v7x, 256 devices: a whole 4x4x8 slice. The times are simulated.
256 devices in a mesh: sample: 32 (over z, x_hi, core), feat: 8 (over x_lo, y).
Axes of the slice: x: 4 (x_hi: 2, x_lo: 2; x = x_hi * 2 + x_lo), y: 4, z: 8, core: 2. Of those that a mesh axis runs over, the one named last changes fastest.
Arguments:
- expression: bfloat16 [8192, 65536], P('sample', 'feat'), may hold values from -6 to 6
- factors: float32 [8192, 256], P('sample'), may hold values from -1.5 to 1.5
- loadings: float32 [65536, 256], P(('feat', 'sample')), may hold values from -1.5 to 1.5
- batch_mask: int32 [2, 5], replicated, may hold values 0 or 1
- modality: int32 [65536], P('feat'), may hold values from 0 to 4, as said below
Outputs:
- factors_out: float32 [8192, 256], P('sample')
- loadings_out: float32 [65536, 256], P(('feat', 'sample'))
Inputs may be any that keep to these rules, and one draw needn't show every extreme that they name: `modality`: modalities 0 to 4 hold 2048, 4096, 6144, 16384 and 36864 features, in a random order.
All inputs are finite; a program needn't handle non-finite values.
Results may differ from a plain program's by a relative error of at most 0.0031.
Values may be sent and summed in bfloat16 or wider, within the bound.
A program may use at most 128 MiB of HBM per device.

v0:
```python
import math

import jax
import jax.numpy as jnp
from jax import lax
from jax.sharding import PartitionSpec as P

ITERS = 2


def per_device(expression, factors, loadings, batch_mask, modality):
    rows = factors.shape[0]
    rank = factors.shape[1]
    cells = rows * lax.axis_size("sample")
    features = expression.shape[1] * lax.axis_size("feat")
    rate_z = 0.9 * math.sqrt(rank) / features
    rate_w = 0.9 * math.sqrt(rank) / cells
    batch_count = batch_mask.shape[0]
    batch_size = cells // batch_count
    which = lax.axis_index("sample") * rows // batch_size
    pick = (jnp.arange(batch_count, dtype=jnp.int32) == which).astype(jnp.float32)
    seen_mods = jnp.sum(pick[:, None] * batch_mask.astype(jnp.float32), axis=0)
    onehot = (
        modality[:, None] == jnp.arange(batch_mask.shape[1], dtype=jnp.int32)[None, :]
    ).astype(jnp.float32)
    observed = jnp.sum(onehot * seen_mods[None, :], axis=1)
    for step in range(ITERS):
        zb = factors.astype(jnp.bfloat16)
        group_w = lax.all_gather(loadings.astype(jnp.bfloat16), "sample", axis=0, tiled=True)
        pred = lax.dot_general(
            zb, group_w, (((1,), (1,)), ((), ())), preferred_element_type=jnp.float32
        )
        resid = (observed[None, :] * (pred - expression.astype(jnp.float32))).astype(jnp.bfloat16)
        partial_z = jnp.dot(resid, group_w, preferred_element_type=jnp.float32)
        total_z = lax.psum(partial_z, "feat")
        factors_next = factors - rate_z * total_z
        grad_w = lax.psum_scatter(
            lax.dot_general(
                resid, zb, (((0,), (0,)), ((), ())), preferred_element_type=jnp.float32
            ),
            "sample",
            scatter_dimension=0,
            tiled=True,
        )
        loadings = loadings - rate_w * grad_w
        factors = factors_next
    return (factors, loadings)


def solution(mesh):
    return jax.shard_map(
        per_device,
        mesh=mesh,
        in_specs=(
            P("sample", "feat"),
            P("sample", None),
            P(("feat", "sample"), None),
            P(),
            P("feat"),
        ),
        out_specs=(P("sample", None), P(("feat", "sample"), None)),
        check_vma=False,
    )
```

profile of v0, /device:TPU:2, one launch (start us, length us, event | category | flops | bytes accessed | tf_op | source)
XLA Modules:
  0.0 684.0 jit_solution(18064587776721609720)
XLA Ops:
  7.2 0.0 all-gather.3.cloned.1.call-start
  7.2 1.6 convert_element_type.36
  8.8 0.0 all-gather.3.cloned.1.call-update
  8.9 0.0 reduce-scatter.3.cloned.1.call-start
  8.9 0.8 multiply_reduce_fusion
  9.7 0.9 select_reduce_fusion
  10.6 89.6 %all-gather.3.cloned.1.call-done = bf16[8192,256]{1,0:T(8,128)(2,1)} async-done(((bf16[256,256]{1,0:T(8,128)(2,1)}), bf16[8192,256]{1,0:T(8,128)(2,1)}) %all-gather.3.cloned.1.call-update) | async-done | bytes 4194320 | tf_op jit(solution)/shard_map/all_gather | solution.py:29
  100.3 4.8 fusion.2
  105.1 1.9 copy-done.1
  107.0 4.6 fusion.6
  111.6 0.0 reduce-scatter.3.cloned.1.call-update
  111.6 0.0 all-reduce.3.cloned.1.call-start
  111.7 5.4 fusion.9
  117.1 0.0 all-reduce.3.cloned.1.call-update
  117.2 0.0 all-gather.5.cloned.1.call-start
  117.2 145.3 %reduce-scatter.3.cloned.1.call-done = f32[256,256]{1,0:T(8,128)} async-done(((f32[8192,256]{1,0:T(8,128)}), f32[256,256]{1,0:T(8,128)}) %reduce-scatter.3.cloned.1.call-update) | async-done | bytes 262160 | tf_op jit(solution)/shard_map/reduce_scatter | solution.py:37
  262.5 1.6 fusion.5
  264.2 0.0 all-gather.5.cloned.1.call-update
  264.2 0.0 all-reduce.5.cloned.1.call-start
  264.2 78.5 %all-reduce.3.cloned.1.call-done = f32[256,256]{1,0:T(8,128)} async-done(((f32[256,256]{1,0:T(8,128)}), f32[256,256]{1,0:T(8,128)}) %all-reduce.3.cloned.1.call-update) | async-done | bytes 262160 | tf_op jit(solution)/shard_map/psum | solution.py:35
  342.8 1.0 fusion.4
  343.8 89.0 %all-gather.5.cloned.1.call-done = bf16[8192,256]{1,0:T(8,128)(2,1)} async-done(((bf16[256,256]{1,0:T(8,128)(2,1)}), bf16[8192,256]{1,0:T(8,128)(2,1)}) %all-gather.5.cloned.1.call-update) | async-done | bytes 4194320 | tf_op jit(solution)/shard_map/all_gather | solution.py:29
  432.8 4.9 fusion.3
  437.7 2.0 copy-done
  439.7 1.9 fusion.10
  441.6 0.0 all-reduce.5.cloned.1.call-update
  441.6 0.0 reduce-scatter.5.cloned.1.call-start
  441.7 6.7 fusion.11
  448.5 69.0 %all-reduce.5.cloned.1.call-done = f32[256,256]{1,0:T(8,128)} async-done(((f32[256,256]{1,0:T(8,128)}), f32[256,256]{1,0:T(8,128)}) %all-reduce.5.cloned.1.call-update) | async-done | bytes 262160 | tf_op jit(solution)/shard_map/psum | solution.py:35
  517.5 1.7 multiply_subtract_fusion.1
  519.2 156.3 %reduce-scatter.5.cloned.1.call-done = f32[256,256]{1,0:T(8,128)} async-done(((f32[8192,256]{1,0:T(8,128)}), f32[256,256]{1,0:T(8,128)}) %reduce-scatter.5.cloned.1.call-update) | async-done | bytes 262160 | tf_op jit(solution)/shard_map/reduce_scatter | solution.py:37
  675.5 1.7 multiply_subtract_fusion
  (14 shorter events, 0.0 us)
Async XLA Ops:
  7.2 93.1 %all-gather.3.cloned.1.call-start = ((), (), s32[]{:S(2)}) async-start(), calls=%async_computation.2 | async-start | bytes 4325376 | tf_op jit(solution)/shard_map/all_gather | solution.py:29
  8.9 253.7 %reduce-scatter.3.cloned.1.call-start = ((), (), s32[]{:S(2)}) async-start(), calls=%async_computation.4 | async-start | bytes 8650752 | tf_op jit(solution)/shard_map/reduce_scatter | solution.py:37
  10.6 96.4 %copy-start.3 = (f32[256,256]{1,0:T(8,128)S(1)}, f32[256,256]{1,0:T(8,128)}, u32[]{:S(2)}) copy-start(f32[256,256]{1,0:T(8,128)} %param.6) | copy-start | bytes 786436
  105.1 1.9 copy-start.1
  111.6 150.9 %copy-start.4 = (f32[256,256]{1,0:T(8,128)S(1)}, f32[256,256]{1,0:T(8,128)}, u32[]{:S(2)}) copy-start(f32[256,256]{1,0:T(8,128)} %param.7) | copy-start | bytes 786436
  111.6 231.1 %all-reduce.3.cloned.1.call-start = ((), (), s32[]{:S(2)}) async-start(), calls=%async_computation.3 | async-start | bytes 524288 | tf_op jit(solution)/shard_map/psum | solution.py:35
  117.2 315.7 %all-gather.5.cloned.1.call-start = ((), (), s32[]{:S(2)}) async-start(), calls=%async_computation.5 | async-start | bytes 4325376 | tf_op jit(solution)/shard_map/all_gather | solution.py:29
  264.2 253.3 %all-reduce.5.cloned.1.call-start = ((), (), s32[]{:S(2)}) async-start(), calls=%async_computation.6 | async-start | bytes 524288 | tf_op jit(solution)/shard_map/psum | solution.py:35
  432.8 6.9 %copy-start.2 = (bf16[8192,256]{1,0:T(8,128)(2,1)S(1)}, bf16[8192,256]{1,0:T(8,128)(2,1)}, u32[]{:S(2)}) copy-start(bf16[8192,256]{1,0:T(8,128)(2,1)} %all-gather.5.cloned.1.call-done) | copy-start | bytes 12582916
  437.7 2.0 copy-start
  441.6 233.8 %reduce-scatter.5.cloned.1.call-start = ((), (), s32[]{:S(2)}) async-start(), calls=%async_computation.7 | async-start | bytes 8650752 | tf_op jit(solution)/shard_map/reduce_scatter | solution.py:37
  448.4 69.0 %copy-start.6 = (f32[256,256]{1,0:T(8,128)S(1)}, f32[256,256]{1,0:T(8,128)}, u32[]{:S(2)}) copy-start(f32[256,256]{1,0:T(8,128)} %all-reduce.3.cloned.1.call-done) | copy-start | bytes 786436
  448.4 227.0 %copy-start.5 = (f32[256,256]{1,0:T(8,128)S(1)}, f32[256,256]{1,0:T(8,128)}, u32[]{:S(2)}) copy-start(f32[256,256]{1,0:T(8,128)} %reduce-scatter.3.cloned.1.call-done) | copy-start | bytes 786436
Sparse Core Ops, SparseCore 0:
  11.4 88.8 all-gather.2
  111.7 150.7 reduce-scatter.2
  265.7 77.0 all-reduce.2
  346.4 86.3 all-gather.4
  441.8 75.6 all-reduce.4
  521.7 153.6 reduce-scatter.4
where the time goes:
time: 685 us; the launch traced here: 684 us
  waiting for transfers between devices  628 us (92%)
  matrix products  28.4 us (4%)
  between operations  14.2 us (2%)
  other arithmetic  9.33 us (1%)
    reduce_scatter x2, waiting for transfers between devices, per_device(): lax.psum_scatter(lax.dot_general(resid, zb, (((0,), (0,)), ((), ())), pre...  302 us
    all_gather x2, waiting for transfers between devices, per_device(): lax.all_gather(loadings.astype(jnp.bfloat16), 'sample', axis=0, tiled=True)  179 us
    psum x2, waiting for transfers between devices, per_device(): total_z = lax.psum(partial_z, 'feat')  148 us
  transfers between devices with their start and end apart: 6, of which 6 were waited for; matrix products, arithmetic and copies ran while one was open for 3% of the time, Pallas kernels for 0%

commit v1 on v0

v1 whole, which is shorter than its diff:
```python
import math

import jax
import jax.numpy as jnp
from jax import lax
from jax.experimental import pallas as pl
from jax.experimental.pallas import tpu as pltpu
from jax.sharding import PartitionSpec as P

ITERS = 2
NZ = 8
NF = 8
T = 256
MODS = 5
BF = jnp.bfloat16
F32 = jnp.float32
STREAMS = ((0, 0), (1, 1), (0, 1), (1, 0))
FULL = ((0, 0), (1, 1))


def nn(a, b):
    return jnp.dot(a, b, preferred_element_type=F32)


def nt(a, b):
    return lax.dot_general(a, b, (((1,), (1,)), ((), ())), preferred_element_type=F32)


def kernel(
    rate_z, rate_w,
    x_hbm, z_in, w_in, mask, modality, z_out, w_out,
    x, obs, zb, zt, zf, wf, wg, own, sib_out, sib_in, ring_out, ring_in, pair_out, pair_in,
    g_local, g_sib, g_half, g_pair, g_z, g_all, pz, z_in_parts, z_new,
    x_sem, ag_s, ag_r, agx_s, agx_r, ags_s, ags_r, rs_s, rs_r, rsx_s, rsx_r, rss_s, rss_r,
    g_s, g_r, gz_s, gz_r, gf_s, gf_r, az_s, az_r, an_s, an_r,
):
    s = lax.axis_index("sample")
    k = lax.axis_index("feat")
    z = s // 4
    xh = (s // 2) % 2
    c = s % 2
    batch = z // 4
    sibling = {"sample": z * 4 + xh * 2 + (1 - c)}
    partner = {"sample": z * 4 + (1 - xh) * 2 + c}

    def along(step):
        return {"sample": ((z + step + NZ) % NZ) * 4 + xh * 2 + c}

    def peer(off):
        return {"feat": (k + off) % NF}

    neighbour = (along(1), along(-1))
    started = []

    def copy(src, dst, send, recv, device):
        return pltpu.make_async_remote_copy(
            src_ref=src, dst_ref=dst, send_sem=send, recv_sem=recv,
            device_id=device, device_id_type=pl.DeviceIdType.MESH,
        )

    def send(*args):
        one = copy(*args)
        one.start()
        started.append(one)

    def shard(rel_z, col, core):
        which = xh if col == 0 else 1 - xh
        return ((z + rel_z + NZ) % NZ) * 4 + which * 2 + core

    load_x = pltpu.make_async_copy(x_hbm, x, x_sem)
    load_x.start()
    zb[0] = z_in[...].astype(BF)
    wf[0] = w_in[...]
    wg[0, s] = w_in[...].astype(BF)

    barrier = pltpu.get_barrier_semaphore()
    greet = [sibling, partner] + [along(d) for d in range(1, NZ)] + [peer(d) for d in range(1, NF)]
    for device in greet:
        pl.semaphore_signal(barrier, inc=1, device_id=device, device_id_type=pl.DeviceIdType.MESH)
    pl.semaphore_wait(barrier, len(greet))

    def ag_hop(it, d, col, t):
        return (d, col) in FULL or t < 3

    def ag_send(it, d, col, t):
        origin = shard(-t if d == 0 else t, col, c)
        block = wg.at[it, origin]
        i = ((it * 2 + d) * 2 + col) * 4 + t
        send(block, block, ag_s.at[i], ag_r.at[i], neighbour[d])

    def ag_sibling(it, rel, col):
        block = wg.at[it, shard(rel, col, c)]
        i = (it * NZ + rel % NZ) * 2 + col
        send(block, block, ags_s.at[i], ags_r.at[i], sibling)

    def ag_begin(it):
        for d in (0, 1):
            ag_send(it, d, 0, 0)
        block = wg.at[it, s]
        send(block, block, agx_s.at[it], agx_r.at[it], partner)
        ag_sibling(it, 0, 0)

    def ag_pair(it):
        block = wg.at[it, shard(0, 1, c)]
        copy(block, block, agx_s.at[it], agx_r.at[it], partner).wait_recv()
        for d in (0, 1):
            ag_send(it, d, 1, 0)
        ag_sibling(it, 0, 1)

    def ag_step(it, t):
        for d, col in ((0, 0), (1, 0), (0, 1), (1, 1)):
            if not ag_hop(it, d, col, t):
                continue
            rel = -(t + 1) if d == 0 else t + 1
            block = wg.at[it, shard(rel, col, c)]
            i = ((it * 2 + d) * 2 + col) * 4 + t
            copy(block, block, ag_s.at[i], ag_r.at[i], neighbour[d]).wait_recv()
            if t < 3 and ag_hop(it, d, col, t + 1):
                ag_send(it, d, col, t + 1)
            ag_sibling(it, rel % NZ, col)

    def ag_from_sibling(it, rel):
        for col in (0, 1):
            block = wg.at[it, shard(rel, col, 1 - c)]
            i = (it * NZ + rel % NZ) * 2 + col
            copy(block, block, ags_s.at[i], ags_r.at[i], sibling).wait_recv()

    def factor_part(it, rel, first=False):
        ag_from_sibling(it, rel)
        there = (z + rel + NZ) % NZ

        def body(j, carry):
            w = wg[it, pl.ds(there * 4 + j * 2, 2)].reshape(2 * T, T)
            cols = pl.ds(pl.multiple_of(there * 4 * T + j * 2 * T, 2 * T), 2 * T)
            pred = nt(zb[it], w)
            resid = (obs[batch, :, cols] * (pred - x[:, cols].astype(F32))).astype(BF)
            pz[it] += nn(resid, w)
            return carry

        if first:
            pz[it] = jnp.zeros((T, T), F32)
        lax.fori_loop(0, 2, body, 0)

    def cross(it, low, high):
        def body(i, carry):
            odd = i % 2
            rel = (4 + i // 2 - odd * (2 * (i // 2) + 1)) % NZ
            there = (z + rel) % NZ
            for col in (0, 1):
                which = xh if col == 0 else 1 - xh
                for mine in (False, True):
                    core = c if mine else 1 - c
                    cols = pl.ds(pl.multiple_of((there * 4 + which * 2 + core) * T, T), T)
                    value = nn(zt[...], x[:, cols]) * obs[batch, :, cols]
                    slot = rel * 2 + col
                    if mine:
                        own[slot] = value
                    else:
                        sib_out[it, slot] = value.astype(BF)
                        sem = it * 2 * NZ + slot
                        copy(
                            sib_out.at[it, slot], sib_in.at[it, slot], rss_s.at[sem], rss_r.at[sem], sibling
                        ).start()
            return carry

        lax.fori_loop(low, high, body, 0)

    def cross_end(it):
        def body(slot, carry):
            sem = it * 2 * NZ + slot
            copy(
                sib_out.at[it, slot], sib_in.at[it, slot], rss_s.at[sem], rss_r.at[sem], sibling
            ).wait_send()
            return carry

        lax.fori_loop(0, 2 * NZ, body, 0)

    def chip_sum(it, rel, col):
        slot = (rel % NZ) * 2 + col
        sem = it * 2 * NZ + slot
        copy(
            sib_out.at[it, slot], sib_in.at[it, slot], rss_s.at[sem], rss_r.at[sem], sibling
        ).wait_recv()
        return own[slot] + sib_in[it, slot].astype(F32)

    def arrived(it, d, col, t):
        i = ((it * 2 + d) * 2 + col) * 4 + t
        copy(ring_out.at[i], ring_in.at[i], rs_s.at[i], rs_r.at[i], neighbour[d]).wait_recv()
        return ring_in[i].astype(F32)

    def rs_step(it, t):
        for d, col in STREAMS:
            if t == 0 and (d, col) not in FULL:
                continue
            value = chip_sum(it, 4 - t if d == 0 else t - 4, col)
            if t > 1 or (t == 1 and (d, col) in FULL):
                value = value + arrived(it, d, col, t - 1)
            i = ((it * 2 + d) * 2 + col) * 4 + t
            ring_out[i] = value.astype(BF)
            send(ring_out.at[i], ring_in.at[i], rs_s.at[i], rs_r.at[i], neighbour[d])

    def rs_pair_send(it):
        value = chip_sum(it, 0, 1) + arrived(it, 0, 1, 3) + arrived(it, 1, 1, 3)
        pair_out[it] = value.astype(BF)
        send(pair_out.at[it], pair_in.at[it], rsx_s.at[it], rsx_r.at[it], partner)

    def rs_end(it):
        value = chip_sum(it, 0, 0) + arrived(it, 0, 0, 3) + arrived(it, 1, 0, 3)
        copy(pair_out.at[it], pair_in.at[it], rsx_s.at[it], rsx_r.at[it], partner).wait_recv()
        return value + pair_in[it].astype(F32)

    half = pl.multiple_of(k * 32 + c * 16, 16)
    other_half = pl.multiple_of(k * 32 + (1 - c) * 16, 16)
    base = pl.multiple_of(k * 32 + c * 16 + xh * 8, 8)
    mine8 = pl.multiple_of(xh * 8, 8)
    other8 = pl.multiple_of((1 - xh) * 8, 8)

    def gram(it):
        zt[...] = zb[it].astype(F32).T.astype(BF)
        g_local[it] = nn(zt[...], zb[it])
        i = it * 4
        send(g_local.at[it, pl.ds(other_half, 16)], g_sib.at[it], g_s.at[i], g_r.at[i], sibling)

    def gram_pair(it):
        i = it * 4
        copy(g_half.at[it], g_sib.at[it], g_s.at[i], g_r.at[i], sibling).wait_recv()
        g_half[it] = g_local[it, pl.ds(half, 16)] + g_sib[it]
        i = it * 4 + 1
        send(g_half.at[it, pl.ds(other8, 8)], g_pair.at[it], g_s.at[i], g_r.at[i], partner)

    def gram_z(it):
        i = it * 4 + 1
        copy(g_pair.at[it], g_pair.at[it], g_s.at[i], g_r.at[i], partner).wait_recv()
        g_z[it, z] = g_half[it, pl.ds(mine8, 8)] + g_pair[it]
        for off in range(1, NZ):
            i = it * NZ + off
            send(g_z.at[it, z], g_z.at[it, z], gz_s.at[i], gz_r.at[i], along(off))

    def gram_batches(it):
        for off in range(1, NZ):
            i = it * NZ + off
            slot = g_z.at[it, (z + NZ - off) % NZ]
            copy(slot, slot, gz_s.at[i], gz_r.at[i], along(off)).wait_recv()
        for b in (0, 1):
            g_all[it, b, pl.ds(base, 8)] = (
                (g_z[it, 4 * b] + g_z[it, 4 * b + 1]) + (g_z[it, 4 * b + 2] + g_z[it, 4 * b + 3])
            )
        block = g_all.at[it, :, pl.ds(base, 8)]
        send(block, block, g_s.at[it * 4 + 2], g_r.at[it * 4 + 2], partner)

    def gram_sibling(it):
        rows = pl.multiple_of(k * 32 + c * 16 + (1 - xh) * 8, 8)
        block = g_all.at[it, :, pl.ds(rows, 8)]
        copy(block, block, g_s.at[it * 4 + 2], g_r.at[it * 4 + 2], partner).wait_recv()
        block = g_all.at[it, :, pl.ds(half, 16)]
        send(block, block, g_s.at[it * 4 + 3], g_r.at[it * 4 + 3], sibling)

    def gram_feat(it):
        block = g_all.at[it, :, pl.ds(other_half, 16)]
        copy(block, block, g_s.at[it * 4 + 3], g_r.at[it * 4 + 3], sibling).wait_recv()
        block = g_all.at[it, :, pl.ds(pl.multiple_of(k * 32, 32), 32)]
        for off in range(1, NF):
            i = it * NF + off
            send(block, block, gf_s.at[i], gf_r.at[i], peer(off))

    def new_loadings(it):
        for off in range(1, NF):
            i = it * NF + off
            rows = pl.multiple_of(((k + NF - off) % NF) * 32, 32)
            block = g_all.at[it, :, pl.ds(rows, 32)]
            copy(block, block, gf_s.at[i], gf_r.at[i], peer(off)).wait_recv()
        cols = pl.ds(pl.multiple_of(s * T, T), T)
        w = wg[it, s]
        grad = jnp.zeros((T, T), F32)
        for b in (0, 1):
            g = g_all[it, b]
            high = g.astype(BF)
            low = (g - high.astype(F32)).astype(BF)
            grad = grad + obs[b, :, cols] * (nt(high, w) + nt(low, w))
        grad = grad - rs_end(it)
        return wf[it] - rate_w * grad.T

    rows32 = pl.multiple_of(k * 32, 32)

    def factors_send(it):
        for off in range(1, NF):
            i = it * NF + off
            rows = pl.multiple_of(((k + off) % NF) * 32, 32)
            send(pz.at[it, pl.ds(rows, 32)], z_in_parts.at[it, off], az_s.at[i], az_r.at[i], peer(off))

    def factors_sum(it):
        total = pz[it, pl.ds(rows32, 32)]
        for off in range(1, NF):
            i = it * NF + off
            slot = z_in_parts.at[it, off]
            copy(slot, slot, az_s.at[i], az_r.at[i], peer(off)).wait_recv()
            total = total + z_in_parts[it, off]
        old = z_in[pl.ds(rows32, 32)] if it == 0 else zf[...]
        new = old - rate_z * total
        if it == 0:
            zf[...] = new
            zb[1, pl.ds(rows32, 32)] = new.astype(BF)
        else:
            z_new[pl.ds(rows32, 32)] = new
        target = zb.at[1] if it == 0 else z_new
        block = target.at[pl.ds(rows32, 32)]
        for off in range(1, NF):
            i = it * NF + off
            send(block, block, an_s.at[i], an_r.at[i], peer(off))

    def factors_wait(it):
        target = zb.at[1] if it == 0 else z_new
        for off in range(1, NF):
            i = it * NF + off
            block = target.at[pl.ds(pl.multiple_of(((k + NF - off) % NF) * 32, 32), 32)]
            copy(block, block, an_s.at[i], an_r.at[i], peer(off)).wait_recv()

    for it in range(ITERS):
        if it == 0:
            ag_begin(0)
            gram(0)
            for b in (0, 1):
                seen = jnp.zeros(modality.shape, F32)
                for m in range(MODS):
                    seen = jnp.where(modality[...] == m, mask[b, m].astype(F32), seen)
                obs[b] = seen
            load_x.wait()
        else:
            factors_sum(0)
            ag_pair(1)
            factors_wait(0)
            gram(1)
        cross(it, 0, 3)
        rs_step(it, 0)
        if it == 0:
            ag_pair(0)
        gram_pair(it)
        cross(it, 3, NZ)
        gram_z(it)
        rs_step(it, 1)
        ag_step(it, 0)
        factor_part(it, 0, first=True)
        gram_batches(it)
        rs_step(it, 2)
        ag_step(it, 1)
        gram_sibling(it)
        factor_part(it, 1)
        factor_part(it, 7)
        rs_step(it, 3)
        ag_step(it, 2)
        gram_feat(it)
        factor_part(it, 2)
        factor_part(it, 6)
        rs_pair_send(it)
        ag_step(it, 3)
        factor_part(it, 3)
        factor_part(it, 5)
        new = new_loadings(it)
        if it == 0:
            wf[1] = new
            wg[1, s] = new.astype(BF)
            ag_begin(1)
            factor_part(it, 4)
            factors_send(it)
        else:
            w_out[...] = new
            factor_part(it, 4)
            factors_send(it)
            factors_sum(it)
            factors_wait(it)
            z_out[...] = z_new[...]

    for one in started:
        one.wait_send()
    for it in range(ITERS):
        cross_end(it)


def per_device(expression, factors, loadings, batch_mask, modality):
    rows = factors.shape[0]
    rank = factors.shape[1]
    cells = rows * lax.axis_size("sample")
    width = expression.shape[1]
    features = width * lax.axis_size("feat")
    rate_z = 0.9 * math.sqrt(rank) / features
    rate_w = 0.9 * math.sqrt(rank) / cells
    vm = pl.BlockSpec(memory_space=pltpu.VMEM)
    dma = lambda n: pltpu.SemaphoreType.DMA((n,))
    out = jax.ShapeDtypeStruct((T, T), F32)

    def body(*refs):
        kernel(rate_z, rate_w, *refs)

    return pl.pallas_call(
        body,
        out_shape=(out, out),
        in_specs=[
            pl.BlockSpec(memory_space=pl.ANY), vm, vm, pl.BlockSpec(memory_space=pltpu.SMEM), vm,
        ],
        out_specs=(vm, vm),
        scratch_shapes=[
            pltpu.VMEM((rows, width), BF),
            pltpu.VMEM((2, 1, width), F32),
            pltpu.VMEM((ITERS, T, T), BF),
            pltpu.VMEM((T, T), BF),
            pltpu.VMEM((32, T), F32),
            pltpu.VMEM((ITERS, T, T), F32),
            pltpu.VMEM((ITERS, 32, T, T), BF),
            pltpu.VMEM((2 * NZ, T, T), F32),
            pltpu.VMEM((ITERS, 2 * NZ, T, T), BF),
            pltpu.VMEM((ITERS, 2 * NZ, T, T), BF),
            pltpu.VMEM((ITERS * 16, T, T), BF),
            pltpu.VMEM((ITERS * 16, T, T), BF),
            pltpu.VMEM((ITERS, T, T), BF),
            pltpu.VMEM((ITERS, T, T), BF),
            pltpu.VMEM((ITERS, T, T), F32),
            pltpu.VMEM((ITERS, 16, T), F32),
            pltpu.VMEM((ITERS, 16, T), F32),
            pltpu.VMEM((ITERS, 8, T), F32),
            pltpu.VMEM((ITERS, NZ, 8, T), F32),
            pltpu.VMEM((ITERS, 2, T, T), F32),
            pltpu.VMEM((ITERS, T, T), F32),
            pltpu.VMEM((ITERS, NF, 32, T), F32),
            pltpu.VMEM((T, T), F32),
            pltpu.SemaphoreType.DMA,
            dma(ITERS * 16), dma(ITERS * 16),
            dma(ITERS), dma(ITERS),
            dma(ITERS * 16), dma(ITERS * 16),
            dma(ITERS * 16), dma(ITERS * 16),
            dma(ITERS), dma(ITERS),
            dma(ITERS * 16), dma(ITERS * 16),
            dma(ITERS * 4), dma(ITERS * 4),
            dma(ITERS * NZ), dma(ITERS * NZ),
            dma(ITERS * NF), dma(ITERS * NF),
            dma(ITERS * NF), dma(ITERS * NF),
            dma(ITERS * NF), dma(ITERS * NF),
        ],
        compiler_params=pltpu.CompilerParams(
            collective_id=0, has_side_effects=True, vmem_limit_bytes=60 * 1024 * 1024
        ),
    )(expression, factors, loadings, batch_mask, modality.reshape(1, width))


def solution(mesh):
    return jax.shard_map(
        per_device,
        mesh=mesh,
        in_specs=(
            P("sample", "feat"),
            P("sample", None),
            P(("feat", "sample"), None),
            P(),
            P("feat"),
        ),
        out_specs=(P("sample", None), P(("feat", "sample"), None)),
        check_vma=False,
    )
```

time: 685 us -> 132 us (0.19)
  waiting for transfers between devices: 628 us -> 0 us
  Pallas kernels: 0 us -> 127 us
  matrix products: 28.4 us -> 0 us
  between operations: 14.2 us -> 0.64 us
  other arithmetic: 9.33 us -> 0 us
    reduce_scatter x2 -> x0, waiting for transfers between devices: 302 us -> none  [per_device(): lax.psum_scatter(lax.dot_general(resid, zb, (((0,), (0,)), ((), ())), pre...]
    all_gather x2 -> x0, waiting for transfers between devices: 179 us -> none  [per_device(): lax.all_gather(loadings.astype(jnp.bfloat16), 'sample', axis=0, tiled=True)]
    psum x2 -> x0, waiting for transfers between devices: 148 us -> none  [per_device(): total_z = lax.psum(partial_z, 'feat')]
    pallas_call x0 -> x1, Pallas kernels: none -> 127 us  [per_device(): pl.pallas_call(body, out_shape=(out, out), in_specs=[pl.BlockSpec(memory_...]
    dot_general x6 -> x0, matrix products: 28.4 us -> none  [the longest x2 11.3 us: per_device(): lax.dot_general(resid, zb, (((0,), (0,)), ((), ())), preferred_element_ty...]
  transfers between devices with their start and end apart: 6 -> 0, of which waited for: 6 -> 0; matrix products, arithmetic and copies ran while one was open for 3% -> 0% of each run, Pallas kernels for 0% -> 0%
where the time goes in v1:
time: 132 us; the launch traced here: 131 us
  Pallas kernels  127 us (96%)
  local copies, waits for them, and re-layouts  3.34 us (3%)
    pallas_call x1, Pallas kernels, per_device(): pl.pallas_call(body, out_shape=(out, out), in_specs=[pl.BlockSpec(memory_...  127 us
    unnamed x2, local copies, waits for them, and re-layouts  3.34 us

profile of v1, /device:TPU:2, one launch (start us, length us, event | category | flops | bytes accessed | tf_op | source)
XLA Modules:
  0.0 131.0 jit_solution(8007673058019877308)
XLA Ops:
  0.6 127.0 %shard_map.68 = (f32[256,256]{1,0:T(8,128)}, f32[256,256]{1,0:T(8,128)}) custom-call(bf16[256,8192]{1,0:T(8,128)(2,1)} %refs_0_.1, f32[256,256]{1,0:T(8,128)} %refs_1_.1, f32[256,256]{1,0:T(8,128)} %refs_2_.1, s32[2,5]{1,0:T(2,128)} %refs_3_.1, s32[1,8192]{1,0:T(1,128)} %bitcast.1), custom_call_target="tpu_custom_call" | custom-call | tf_op jit(solution)/shard_map/pallas_call | solution.py:394
  127.7 1.7 %copy.9 = f32[256,256]{1,0:T(8,128)} copy(f32[256,256]{1,0:T(8,128)} %get-tuple-element.4) | data formatting | bytes 524288
  129.3 1.7 %copy.10 = f32[256,256]{1,0:T(8,128)} copy(f32[256,256]{1,0:T(8,128)} %get-tuple-element.5) | data formatting | bytes 524288

commit v2 on v1

v2 whole, which is shorter than its diff:
```python
import math

import jax
import jax.numpy as jnp
from jax import lax
from jax.experimental import pallas as pl
from jax.experimental.pallas import tpu as pltpu
from jax.sharding import PartitionSpec as P

ITERS = 2
NZ = 8
NF = 8
T = 256
MODS = 5
BF = jnp.bfloat16
F32 = jnp.float32
H = T // 2
KINDS = ((0, 0), (0, 1), (1, 1))
AG_FULL = ((0, 0), (0, 1), (1, 2))
RS_FULL = ((1, 0), (1, 1), (0, 2))
ORDER = (
    ("agb", 0), ("gram", 0), ("ld",), ("cr", 0, 4), ("cr", 0, 3), ("cr", 0, 5), ("cr", 0, 2), ("agp", 0),
    ("rs", 0, 1, 1, 0), ("rx", 0, 4), ("rs", 0, 0, 2, 0), ("ag", 0, 0, 0, 0), ("ag", 0, 1, 0, 0),
    ("rs", 0, 0, 1, 1), ("rx", 0, 3), ("cr", 0, 6), ("ag", 0, 0, 1, 0), ("ag", 0, 1, 1, 0), ("rx", 0, 5),
    ("rs", 0, 1, 2, 1), ("cr", 0, 1), ("rx", 0, 2), ("rs", 0, 1, 0, 0), ("ag", 0, 0, 2, 0), ("ag", 0, 1, 2, 0),
    ("cr", 0, 7), ("cr", 0, 0), ("rx", 0, 6), ("rs", 0, 0, 2, 1), ("rs", 0, 1, 1, 1), ("gp", 0), ("agc", 0, 0),
    ("agc", 0, 7), ("agc", 0, 1), ("ag", 0, 0, 0, 1), ("ag", 0, 1, 0, 1), ("rx", 0, 1), ("rs", 0, 0, 0, 1),
    ("ag", 0, 1, 1, 1), ("rs", 0, 0, 1, 2), ("rx", 0, 7), ("rx", 0, 0), ("ag", 0, 0, 1, 1), ("rs", 0, 1, 2, 2),
    ("fp", 0, 0), ("ag", 0, 0, 2, 1), ("rs", 0, 1, 0, 1), ("fp", 0, 7), ("ag", 0, 1, 2, 1), ("rs", 0, 0, 2, 2),
    ("gz", 0), ("fp", 0, 1), ("ag", 0, 0, 0, 2), ("rs", 0, 1, 1, 2), ("agc", 0, 6), ("ag", 0, 1, 0, 2),
    ("rs", 0, 0, 0, 2), ("agc", 0, 2), ("fp", 0, 6), ("ag", 0, 1, 1, 2), ("rs", 0, 0, 1, 3), ("fp", 0, 2),
    ("ag", 0, 0, 1, 2), ("rs", 0, 1, 2, 3), ("ag", 0, 0, 2, 2), ("rs", 0, 1, 0, 2), ("agc", 0, 5),
    ("ag", 0, 1, 2, 2), ("rs", 0, 0, 2, 3), ("gb", 0), ("fp", 0, 5), ("agc", 0, 3), ("ag", 0, 0, 0, 3),
    ("rs", 0, 1, 1, 3), ("gs", 0), ("fp", 0, 3), ("rs", 0, 0, 0, 3), ("gf", 0), ("rs", 0, 1, 0, 3),
    ("agc", 0, 4), ("ag", 0, 0, 1, 3), ("ag", 0, 1, 2, 3), ("rp", 0), ("fp", 0, 4), ("fs", 0), ("nl", 0),
    ("agb", 1), ("fsum", 0), ("agp", 1), ("ag", 1, 0, 0, 0), ("ag", 1, 1, 0, 0), ("agc", 1, 0), ("fw", 0),
    ("gram", 1), ("ag", 1, 0, 1, 0), ("ag", 1, 1, 1, 0), ("fp", 1, 0), ("ag", 1, 0, 2, 0), ("ag", 1, 1, 2, 0),
    ("agc", 1, 7), ("gp", 1), ("cr", 1, 4), ("cr", 1, 3), ("ag", 1, 0, 0, 1), ("ag", 1, 1, 0, 1), ("fp", 1, 7),
    ("ag", 1, 0, 1, 1), ("ag", 1, 1, 1, 1), ("gz", 1), ("rx", 1, 4), ("rx", 1, 3), ("ag", 1, 0, 2, 1),
    ("ag", 1, 1, 2, 1), ("rs", 1, 1, 1, 0), ("rs", 1, 0, 2, 0), ("rs", 1, 0, 1, 1), ("agc", 1, 1),
    ("agc", 1, 6), ("ag", 1, 0, 0, 2), ("ag", 1, 1, 0, 2), ("agc", 1, 2), ("cr", 1, 5), ("fp", 1, 1),
    ("ag", 1, 0, 1, 2), ("ag", 1, 1, 1, 2), ("fp", 1, 6), ("gb", 1), ("ag", 1, 0, 2, 2), ("ag", 1, 1, 2, 2),
    ("rx", 1, 5), ("fp", 1, 2), ("rs", 1, 1, 0, 0), ("rs", 1, 0, 0, 1), ("rs", 1, 1, 2, 1), ("rs", 1, 0, 2, 1),
    ("gs", 1), ("rs", 1, 1, 1, 1), ("agc", 1, 5), ("agc", 1, 3), ("cr", 1, 2), ("cr", 1, 6),
    ("ag", 1, 0, 0, 3), ("ag", 1, 1, 2, 3), ("fp", 1, 5), ("ag", 1, 0, 1, 3), ("fp", 1, 3), ("rx", 1, 2),
    ("rx", 1, 6), ("rs", 1, 1, 0, 1), ("rs", 1, 0, 1, 2), ("rs", 1, 1, 2, 2), ("gf", 1), ("rs", 1, 0, 2, 2),
    ("rs", 1, 1, 1, 2), ("agc", 1, 4), ("cr", 1, 1), ("cr", 1, 7), ("rs", 1, 0, 0, 2), ("fp", 1, 4), ("fs", 1),
    ("rx", 1, 1), ("rs", 1, 1, 0, 2), ("rs", 1, 0, 1, 3), ("cr", 1, 0), ("rx", 1, 7), ("rs", 1, 1, 2, 3),
    ("rs", 1, 0, 2, 3), ("rs", 1, 1, 1, 3), ("rx", 1, 0), ("rs", 1, 0, 0, 3), ("rs", 1, 1, 0, 3), ("fsum", 1),
    ("rp", 1), ("nl", 1), ("fw", 1),
)


def nn(a, b):
    return jnp.dot(a, b, preferred_element_type=F32)


def nt(a, b):
    return lax.dot_general(a, b, (((1,), (1,)), ((), ())), preferred_element_type=F32)


def kernel(
    rate_z, rate_w,
    x_hbm, z_hbm, w_hbm, mask, modality_hbm, z_out, w_out,
    x, obs, zb, zt, zf, wf, wg, own, sib_out, sib_in, ring_out, ring_in, x_out, x_in, pair_out, pair_in,
    g_local, g_sib, g_half, g_pair, g_z, g_all, pz, z_in_parts, z_new,
    z_in, w_in, w_new, modality, x_sem, in_sem, out_sem, ag_s, ag_r, agx_s, agx_r, ags_s, ags_r, rs_s, rs_r, rsa_s, rsa_r, rsx_s, rsx_r, rss_s, rss_r,
    g_s, g_r, gz_s, gz_r, gf_s, gf_r, az_s, az_r, an_s, an_r,
):
    s = lax.axis_index("sample")
    k = lax.axis_index("feat")
    z = s // 4
    xh = (s // 2) % 2
    c = s % 2
    batch = z // 4
    sibling = {"sample": z * 4 + xh * 2 + (1 - c)}
    partner = {"sample": z * 4 + (1 - xh) * 2 + c}

    def along(step):
        return {"sample": ((z + step + NZ) % NZ) * 4 + xh * 2 + c}

    def peer(off):
        return {"feat": (k + off) % NF}

    neighbour = (along(1), along(-1))
    started = []

    def copy(src, dst, send, recv, device):
        return pltpu.make_async_remote_copy(
            src_ref=src, dst_ref=dst, send_sem=send, recv_sem=recv,
            device_id=device, device_id_type=pl.DeviceIdType.MESH,
        )

    def send(*args):
        one = copy(*args)
        one.start()
        started.append(one)

    def shard(rel_z, col, core):
        which = xh if col == 0 else 1 - xh
        return ((z + rel_z + NZ) % NZ) * 4 + which * 2 + core

    load_x = pltpu.make_async_copy(x_hbm, x, x_sem)
    loads = [
        pltpu.make_async_copy(there, here, in_sem.at[i])
        for i, (there, here) in enumerate(((w_hbm, w_in), (z_hbm, z_in), (modality_hbm, modality)))
    ]
    for one in loads:
        one.start()
    load_x.start()

    barrier = pltpu.get_barrier_semaphore()
    greet = [sibling, partner] + [along(d) for d in range(1, NZ)] + [peer(d) for d in range(1, NF)]
    for device in greet:
        pl.semaphore_signal(barrier, inc=1, device_id=device, device_id_type=pl.DeviceIdType.MESH)
    loads[0].wait()
    wg[0, s] = w_in[...].astype(BF)
    loads[1].wait()
    zb[0] = z_in[...].astype(BF)
    loads[2].wait()
    pl.semaphore_wait(barrier, len(greet))

    waited = set()

    def once(key, copies):
        if key not in waited:
            waited.add(key)
            copies().wait_recv()

    def rows(h):
        return pl.ds(h * H, H)

    def ag_send(it, d, kind, t):
        col, h = KINDS[kind]
        block = wg.at[it, shard(-t if d == 0 else t, col, c), rows(h)]
        i = ((it * 2 + d) * 3 + kind) * 4 + t
        send(block, block, ag_s.at[i], ag_r.at[i], neighbour[d])

    def ag_sibling(it, rel, col, h):
        block = wg.at[it, shard(rel, col, c), rows(h)]
        i = ((it * NZ + rel % NZ) * 2 + col) * 2 + h
        send(block, block, ags_s.at[i], ags_r.at[i], sibling)

    def ag_across(it, rel, h):
        block = wg.at[it, shard(rel, 0, c), rows(h)]
        i = it * (NZ + 1) + (NZ if h else rel % NZ)
        send(block, block, agx_s.at[i], agx_r.at[i], partner)

    def ag_begin(it):
        for kind in (0, 1):
            for d in (0, 1):
                ag_send(it, d, kind, 0)
        ag_across(it, 0, 1)
        ag_across(it, 0, 0)
        ag_sibling(it, 0, 0, 0)
        ag_sibling(it, 0, 0, 1)

    def ag_pair(it):
        block = wg.at[it, shard(0, 1, c), rows(1)]
        i = it * (NZ + 1) + NZ
        copy(block, block, agx_s.at[i], agx_r.at[i], partner).wait_recv()
        for d in (0, 1):
            ag_send(it, d, 2, 0)
        ag_sibling(it, 0, 1, 1)

    def ag_one(it, d, kind, t):
        col, h = KINDS[kind]
        full = (d, kind) in AG_FULL
        rel = -(t + 1) if d == 0 else t + 1
        block = wg.at[it, shard(rel, col, c), rows(h)]
        i = ((it * 2 + d) * 3 + kind) * 4 + t
        copy(block, block, ag_s.at[i], ag_r.at[i], neighbour[d]).wait_recv()
        if t < 2 or (t == 2 and full):
            ag_send(it, d, kind, t + 1)
        if kind == 0:
            ag_across(it, rel, 0)
        ag_sibling(it, rel, col, h)

    def ag_crossed(it, rel):
        block = wg.at[it, shard(rel, 1, c), rows(0)]
        i = it * (NZ + 1) + rel % NZ
        copy(block, block, agx_s.at[i], agx_r.at[i], partner).wait_recv()
        ag_sibling(it, rel, 1, 0)

    def ag_from_sibling(it, rel):
        for col, h in ((0, 0), (0, 1), (1, 1), (1, 0)):
            block = wg.at[it, shard(rel, col, 1 - c), rows(h)]
            i = ((it * NZ + rel % NZ) * 2 + col) * 2 + h
            copy(block, block, ags_s.at[i], ags_r.at[i], sibling).wait_recv()

    def factor_part(it, rel):
        ag_from_sibling(it, rel)
        first = ("pz", it) not in waited
        waited.add(("pz", it))
        there = (z + rel + NZ) % NZ

        def body(j, carry):
            w = wg[it, pl.ds(there * 4 + j * 2, 2)].reshape(2 * T, T)
            cols = pl.ds(pl.multiple_of(there * 4 * T + j * 2 * T, 2 * T), 2 * T)
            pred = nt(zb[it], w)
            resid = (obs[batch, :, cols] * (pred - x[:, cols].astype(F32))).astype(BF)
            pz[it] += nn(resid, w)
            return carry

        if first:
            pz[it] = jnp.zeros((T, T), F32)
        lax.fori_loop(0, 2, body, 0)

    def cross(it, rel):
        there = (z + rel) % NZ

        def body(col, carry):
            which = (xh + col) % 2
            slot = rel * 2 + col
            for mine in (False, True):
                core = c if mine else 1 - c
                cols = pl.ds(pl.multiple_of((there * 4 + which * 2 + core) * T, T), T)
                value = nn(zt[...], x[:, cols]) * obs[batch, :, cols]
                if mine:
                    own[slot] = value
                else:
                    sib_out[it, slot] = value.astype(BF)
                    sem = it * 2 * NZ + slot
                    copy(
                        sib_out.at[it, slot], sib_in.at[it, slot], rss_s.at[sem], rss_r.at[sem], sibling
                    ).start()
            return carry

        lax.fori_loop(0, 2, body, 0)

    def cross_end(it):
        def body(slot, carry):
            sem = it * 2 * NZ + slot
            copy(
                sib_out.at[it, slot], sib_in.at[it, slot], rss_s.at[sem], rss_r.at[sem], sibling
            ).wait_send()
            return carry

        lax.fori_loop(0, 2 * NZ, body, 0)

    def chip_sum(it, rel, col, h):
        slot = (rel % NZ) * 2 + col
        sem = it * 2 * NZ + slot
        once(("sib", it, slot), lambda: copy(
            sib_out.at[it, slot], sib_in.at[it, slot], rss_s.at[sem], rss_r.at[sem], sibling
        ))
        value = own[slot, rows(h)] + sib_in[it, slot, rows(h)].astype(F32)
        if col == 0 and h == 0:
            i = it * NZ + rel % NZ
            once(("x", it, rel % NZ), lambda: copy(
                x_out.at[i], x_in.at[i], rsa_s.at[i], rsa_r.at[i], partner
            ))
            value = value + x_in[i].astype(F32)
        return value

    def rs_across(it, rel):
        i = it * NZ + rel
        x_out[i] = chip_sum(it, rel, 1, 0).astype(BF)
        send(x_out.at[i], x_in.at[i], rsa_s.at[i], rsa_r.at[i], partner)

    def arrived(it, d, kind, t):
        i = ((it * 2 + d) * 3 + kind) * 4 + t
        copy(ring_out.at[i], ring_in.at[i], rs_s.at[i], rs_r.at[i], neighbour[d]).wait_recv()
        return ring_in[i].astype(F32)

    def rs_one(it, d, kind, t):
        col, h = KINDS[kind]
        value = chip_sum(it, 4 - t if d == 0 else t - 4, col, h)
        if t > 1 or (t == 1 and (d, kind) in RS_FULL):
            value = value + arrived(it, d, kind, t - 1)
        i = ((it * 2 + d) * 3 + kind) * 4 + t
        ring_out[i] = value.astype(BF)
        send(ring_out.at[i], ring_in.at[i], rs_s.at[i], rs_r.at[i], neighbour[d])

    def rs_pair_send(it):
        value = chip_sum(it, 0, 1, 1) + arrived(it, 0, 2, 3) + arrived(it, 1, 2, 3)
        pair_out[it] = value.astype(BF)
        send(pair_out.at[it], pair_in.at[it], rsx_s.at[it], rsx_r.at[it], partner)

    def rs_end(it):
        low = chip_sum(it, 0, 0, 0) + arrived(it, 0, 0, 3) + arrived(it, 1, 0, 3)
        high = chip_sum(it, 0, 0, 1) + arrived(it, 0, 1, 3) + arrived(it, 1, 1, 3)
        copy(pair_out.at[it], pair_in.at[it], rsx_s.at[it], rsx_r.at[it], partner).wait_recv()
        return jnp.concatenate([low, high + pair_in[it].astype(F32)], axis=0)

    half = pl.multiple_of(k * 32 + c * 16, 16)
    other_half = pl.multiple_of(k * 32 + (1 - c) * 16, 16)
    base = pl.multiple_of(k * 32 + c * 16 + xh * 8, 8)
    mine8 = pl.multiple_of(xh * 8, 8)
    other8 = pl.multiple_of((1 - xh) * 8, 8)

    def gram(it):
        zt[...] = zb[it].astype(F32).T.astype(BF)
        g_local[it] = nn(zt[...], zb[it])
        i = it * 4
        send(g_local.at[it, pl.ds(other_half, 16)], g_sib.at[it], g_s.at[i], g_r.at[i], sibling)

    def gram_pair(it):
        i = it * 4
        copy(g_half.at[it], g_sib.at[it], g_s.at[i], g_r.at[i], sibling).wait_recv()
        g_half[it] = g_local[it, pl.ds(half, 16)] + g_sib[it]
        i = it * 4 + 1
        send(g_half.at[it, pl.ds(other8, 8)], g_pair.at[it], g_s.at[i], g_r.at[i], partner)

    def gram_z(it):
        i = it * 4 + 1
        copy(g_pair.at[it], g_pair.at[it], g_s.at[i], g_r.at[i], partner).wait_recv()
        g_z[it, z] = g_half[it, pl.ds(mine8, 8)] + g_pair[it]
        for off in range(1, NZ):
            i = it * NZ + off
            send(g_z.at[it, z], g_z.at[it, z], gz_s.at[i], gz_r.at[i], along(off))

    def gram_batches(it):
        for off in range(1, NZ):
            i = it * NZ + off
            slot = g_z.at[it, (z + NZ - off) % NZ]
            copy(slot, slot, gz_s.at[i], gz_r.at[i], along(off)).wait_recv()
        for b in (0, 1):
            g_all[it, b, pl.ds(base, 8)] = (
                (g_z[it, 4 * b] + g_z[it, 4 * b + 1]) + (g_z[it, 4 * b + 2] + g_z[it, 4 * b + 3])
            )
        block = g_all.at[it, :, pl.ds(base, 8)]
        send(block, block, g_s.at[it * 4 + 2], g_r.at[it * 4 + 2], partner)

    def gram_sibling(it):
        rows = pl.multiple_of(k * 32 + c * 16 + (1 - xh) * 8, 8)
        block = g_all.at[it, :, pl.ds(rows, 8)]
        copy(block, block, g_s.at[it * 4 + 2], g_r.at[it * 4 + 2], partner).wait_recv()
        block = g_all.at[it, :, pl.ds(half, 16)]
        send(block, block, g_s.at[it * 4 + 3], g_r.at[it * 4 + 3], sibling)

    def gram_feat(it):
        block = g_all.at[it, :, pl.ds(other_half, 16)]
        copy(block, block, g_s.at[it * 4 + 3], g_r.at[it * 4 + 3], sibling).wait_recv()
        block = g_all.at[it, :, pl.ds(pl.multiple_of(k * 32, 32), 32)]
        for off in range(1, NF):
            i = it * NF + off
            send(block, block, gf_s.at[i], gf_r.at[i], peer(off))

    def new_loadings(it):
        for off in range(1, NF):
            i = it * NF + off
            rows = pl.multiple_of(((k + NF - off) % NF) * 32, 32)
            block = g_all.at[it, :, pl.ds(rows, 32)]
            copy(block, block, gf_s.at[i], gf_r.at[i], peer(off)).wait_recv()
        cols = pl.ds(pl.multiple_of(s * T, T), T)
        w = wg[it, s]
        grad = jnp.zeros((T, T), F32)
        for b in (0, 1):
            g = g_all[it, b]
            high = g.astype(BF)
            low = (g - high.astype(F32)).astype(BF)
            grad = grad + obs[b, :, cols] * (nt(high, w) + nt(low, w))
        grad = grad - rs_end(it)
        new = (w_in[...] if it == 0 else wf[...]) - rate_w * grad.T
        if it == 0:
            wf[...] = new
            wg[1, s] = new.astype(BF)
        else:
            w_new[...] = new
            pltpu.make_async_copy(w_new, w_out, out_sem.at[0]).start()

    rows32 = pl.multiple_of(k * 32, 32)

    def factors_send(it):
        for off in range(1, NF):
            i = it * NF + off
            rows = pl.multiple_of(((k + off) % NF) * 32, 32)
            send(pz.at[it, pl.ds(rows, 32)], z_in_parts.at[it, off], az_s.at[i], az_r.at[i], peer(off))

    def factors_sum(it):
        total = pz[it, pl.ds(rows32, 32)]
        for off in range(1, NF):
            i = it * NF + off
            slot = z_in_parts.at[it, off]
            copy(slot, slot, az_s.at[i], az_r.at[i], peer(off)).wait_recv()
            total = total + z_in_parts[it, off]
        old = z_in[pl.ds(rows32, 32)] if it == 0 else zf[...]
        new = old - rate_z * total
        if it == 0:
            zf[...] = new
            zb[1, pl.ds(rows32, 32)] = new.astype(BF)
        else:
            z_new[pl.ds(rows32, 32)] = new
        target = zb.at[1] if it == 0 else z_new
        block = target.at[pl.ds(rows32, 32)]
        for off in range(1, NF):
            i = it * NF + off
            send(block, block, an_s.at[i], an_r.at[i], peer(off))

    def factors_wait(it):
        target = zb.at[1] if it == 0 else z_new
        for off in range(1, NF):
            i = it * NF + off
            block = target.at[pl.ds(pl.multiple_of(((k + NF - off) % NF) * 32, 32), 32)]
            copy(block, block, an_s.at[i], an_r.at[i], peer(off)).wait_recv()
        if it == 1:
            pltpu.make_async_copy(z_new, z_out, out_sem.at[1]).start()

    def load():
        for b in (0, 1):
            seen = jnp.zeros(modality.shape, F32)
            for m in range(MODS):
                seen = jnp.where(modality[...] == m, mask[b, m].astype(F32), seen)
            obs[b] = seen
        load_x.wait()

    do = {
        "agb": ag_begin, "agp": ag_pair, "ag": ag_one, "agc": ag_crossed, "fp": factor_part,
        "fs": factors_send, "fsum": factors_sum, "fw": factors_wait,
        "gram": gram, "gp": gram_pair, "gz": gram_z, "gb": gram_batches, "gs": gram_sibling, "gf": gram_feat,
        "cr": cross, "rx": rs_across, "rs": rs_one, "rp": rs_pair_send, "nl": new_loadings, "ld": load,
    }
    for name, *where in ORDER:
        do[name](*where)

    for one in started:
        one.wait_send()
    for it in range(ITERS):
        cross_end(it)
    pltpu.make_async_copy(w_new, w_out, out_sem.at[0]).wait()
    pltpu.make_async_copy(z_new, z_out, out_sem.at[1]).wait()


def hand_over(z_from, w_from, z_to, w_to):
    z_to[...] = z_from[...]
    w_to[...] = w_from[...]


def per_device(expression, factors, loadings, batch_mask, modality):
    rows = factors.shape[0]
    rank = factors.shape[1]
    cells = rows * lax.axis_size("sample")
    width = expression.shape[1]
    features = width * lax.axis_size("feat")
    rate_z = 0.9 * math.sqrt(rank) / features
    rate_w = 0.9 * math.sqrt(rank) / cells
    hbm = pl.BlockSpec(memory_space=pl.ANY)
    vm = pl.BlockSpec(memory_space=pltpu.VMEM)
    dma = lambda n: pltpu.SemaphoreType.DMA((n,))
    out = jax.ShapeDtypeStruct((T, T), F32)

    def body(*refs):
        kernel(rate_z, rate_w, *refs)

    z_out, w_out = pl.pallas_call(
        body,
        out_shape=(out, out),
        in_specs=[
            hbm, hbm, hbm, pl.BlockSpec(memory_space=pltpu.SMEM), hbm,
        ],
        out_specs=(hbm, hbm),
        scratch_shapes=[
            pltpu.VMEM((rows, width), BF),
            pltpu.VMEM((2, 1, width), F32),
            pltpu.VMEM((ITERS, T, T), BF),
            pltpu.VMEM((T, T), BF),
            pltpu.VMEM((32, T), F32),
            pltpu.VMEM((T, T), F32),
            pltpu.VMEM((ITERS, 32, T, T), BF),
            pltpu.VMEM((2 * NZ, T, T), F32),
            pltpu.VMEM((ITERS, 2 * NZ, T, T), BF),
            pltpu.VMEM((ITERS, 2 * NZ, T, T), BF),
            pltpu.VMEM((ITERS * 24, H, T), BF),
            pltpu.VMEM((ITERS * 24, H, T), BF),
            pltpu.VMEM((ITERS * NZ, H, T), BF),
            pltpu.VMEM((ITERS * NZ, H, T), BF),
            pltpu.VMEM((ITERS, H, T), BF),
            pltpu.VMEM((ITERS, H, T), BF),
            pltpu.VMEM((ITERS, T, T), F32),
            pltpu.VMEM((ITERS, 16, T), F32),
            pltpu.VMEM((ITERS, 16, T), F32),
            pltpu.VMEM((ITERS, 8, T), F32),
            pltpu.VMEM((ITERS, NZ, 8, T), F32),
            pltpu.VMEM((ITERS, 2, T, T), F32),
            pltpu.VMEM((ITERS, T, T), F32),
            pltpu.VMEM((ITERS, NF, 32, T), F32),
            pltpu.VMEM((T, T), F32),
            pltpu.VMEM((T, T), F32),
            pltpu.VMEM((T, T), F32),
            pltpu.VMEM((T, T), F32),
            pltpu.VMEM((1, width), jnp.int32),
            pltpu.SemaphoreType.DMA,
            dma(3), dma(2),
            dma(ITERS * 24), dma(ITERS * 24),
            dma(ITERS * (NZ + 1)), dma(ITERS * (NZ + 1)),
            dma(ITERS * 32), dma(ITERS * 32),
            dma(ITERS * 24), dma(ITERS * 24),
            dma(ITERS * NZ), dma(ITERS * NZ),
            dma(ITERS), dma(ITERS),
            dma(ITERS * 16), dma(ITERS * 16),
            dma(ITERS * 4), dma(ITERS * 4),
            dma(ITERS * NZ), dma(ITERS * NZ),
            dma(ITERS * NF), dma(ITERS * NF),
            dma(ITERS * NF), dma(ITERS * NF),
            dma(ITERS * NF), dma(ITERS * NF),
        ],
        compiler_params=pltpu.CompilerParams(
            collective_id=0, has_side_effects=True, vmem_limit_bytes=60 * 1024 * 1024
        ),
    )(expression, factors, loadings, batch_mask, modality.reshape(1, width))
    return pl.pallas_call(
        hand_over,
        out_shape=(out, out),
        in_specs=[vm, vm],
        out_specs=(vm, vm),
    )(z_out, w_out)


def solution(mesh):
    return jax.shard_map(
        per_device,
        mesh=mesh,
        in_specs=(
            P("sample", "feat"),
            P("sample", None),
            P(("feat", "sample"), None),
            P(),
            P("feat"),
        ),
        out_specs=(P("sample", None), P(("feat", "sample"), None)),
        check_vma=False,
    )
```

time: 132 us -> 111 us (0.84)
  Pallas kernels: 127 us -> 109 us
  local copies, waits for them, and re-layouts: 3.34 us -> 0 us
    pallas_call x1 -> x2, Pallas kernels: 127 us -> 109 us  [the longest x1 107 us: per_device(): pl.pallas_call(body, out_shape=(out, out), in_specs=[hbm, hbm, hbm, pl.Bl...]
    unnamed x2 -> x0, local copies, waits for them, and re-layouts: 3.34 us -> none
where the time goes in v2:
time: 111 us; the launch traced here: 110 us
  Pallas kernels  109 us (98%)
    pallas_call x1, Pallas kernels, per_device(): pl.pallas_call(body, out_shape=(out, out), in_specs=[hbm, hbm, hbm, pl.Bl...  107 us

profile of v2, /device:TPU:2, one launch (start us, length us, event | category | flops | bytes accessed | tf_op | source)
XLA Modules:
  0.0 110.0 jit_solution(1468488103576158464)
XLA Ops:
  0.6 107.5 %shard_map.68 = (f32[256,256]{1,0:T(8,128)}, f32[256,256]{1,0:T(8,128)}) custom-call(bf16[256,8192]{1,0:T(8,128)(2,1)} %refs_0_.1, f32[256,256]{1,0:T(8,128)} %refs_1_.1, f32[256,256]{1,0:T(8,128)} %refs_2_.1, s32[2,5]{1,0:T(2,128)} %refs_3_.1, s32[1,8192]{1,0:T(1,128)} %bitcast.1), custom_call_target="tpu_custom_call" | custom-call | tf_op jit(solution)/shard_map/pallas_call | solution.py:446
  108.1 1.8 %shard_map.69 = (f32[256,256]{1,0:T(8,128)}, f32[256,256]{1,0:T(8,128)}) custom-call(f32[256,256]{1,0:T(8,128)} %get-tuple-element.4.z_from, f32[256,256]{1,0:T(8,128)} %get-tuple-element.5.w_from), custom_call_target="tpu_custom_call" | custom-call | tf_op jit(solution)/shard_map/pallas_call | solution.py:502

commit v3 on v2

--- a/solution.py
+++ b/solution.py
@@ -9,7 +9,6 @@
 
 ITERS = 2
 NZ = 8
-NF = 8
 T = 256
 MODS = 5
 BF = jnp.bfloat16
@@ -19,35 +18,37 @@
 AG_FULL = ((0, 0), (0, 1), (1, 2))
 RS_FULL = ((1, 0), (1, 1), (0, 2))
 ORDER = (
-    ("agb", 0), ("gram", 0), ("ld",), ("cr", 0, 4), ("cr", 0, 3), ("cr", 0, 5), ("cr", 0, 2), ("agp", 0),
-    ("rs", 0, 1, 1, 0), ("rx", 0, 4), ("rs", 0, 0, 2, 0), ("ag", 0, 0, 0, 0), ("ag", 0, 1, 0, 0),
-    ("rs", 0, 0, 1, 1), ("rx", 0, 3), ("cr", 0, 6), ("ag", 0, 0, 1, 0), ("ag", 0, 1, 1, 0), ("rx", 0, 5),
-    ("rs", 0, 1, 2, 1), ("cr", 0, 1), ("rx", 0, 2), ("rs", 0, 1, 0, 0), ("ag", 0, 0, 2, 0), ("ag", 0, 1, 2, 0),
-    ("cr", 0, 7), ("cr", 0, 0), ("rx", 0, 6), ("rs", 0, 0, 2, 1), ("rs", 0, 1, 1, 1), ("gp", 0), ("agc", 0, 0),
-    ("agc", 0, 7), ("agc", 0, 1), ("ag", 0, 0, 0, 1), ("ag", 0, 1, 0, 1), ("rx", 0, 1), ("rs", 0, 0, 0, 1),
-    ("ag", 0, 1, 1, 1), ("rs", 0, 0, 1, 2), ("rx", 0, 7), ("rx", 0, 0), ("ag", 0, 0, 1, 1), ("rs", 0, 1, 2, 2),
-    ("fp", 0, 0), ("ag", 0, 0, 2, 1), ("rs", 0, 1, 0, 1), ("fp", 0, 7), ("ag", 0, 1, 2, 1), ("rs", 0, 0, 2, 2),
-    ("gz", 0), ("fp", 0, 1), ("ag", 0, 0, 0, 2), ("rs", 0, 1, 1, 2), ("agc", 0, 6), ("ag", 0, 1, 0, 2),
-    ("rs", 0, 0, 0, 2), ("agc", 0, 2), ("fp", 0, 6), ("ag", 0, 1, 1, 2), ("rs", 0, 0, 1, 3), ("fp", 0, 2),
-    ("ag", 0, 0, 1, 2), ("rs", 0, 1, 2, 3), ("ag", 0, 0, 2, 2), ("rs", 0, 1, 0, 2), ("agc", 0, 5),
-    ("ag", 0, 1, 2, 2), ("rs", 0, 0, 2, 3), ("gb", 0), ("fp", 0, 5), ("agc", 0, 3), ("ag", 0, 0, 0, 3),
-    ("rs", 0, 1, 1, 3), ("gs", 0), ("fp", 0, 3), ("rs", 0, 0, 0, 3), ("gf", 0), ("rs", 0, 1, 0, 3),
-    ("agc", 0, 4), ("ag", 0, 0, 1, 3), ("ag", 0, 1, 2, 3), ("rp", 0), ("fp", 0, 4), ("fs", 0), ("nl", 0),
-    ("agb", 1), ("fsum", 0), ("agp", 1), ("ag", 1, 0, 0, 0), ("ag", 1, 1, 0, 0), ("agc", 1, 0), ("fw", 0),
-    ("gram", 1), ("ag", 1, 0, 1, 0), ("ag", 1, 1, 1, 0), ("fp", 1, 0), ("ag", 1, 0, 2, 0), ("ag", 1, 1, 2, 0),
-    ("agc", 1, 7), ("gp", 1), ("cr", 1, 4), ("cr", 1, 3), ("ag", 1, 0, 0, 1), ("ag", 1, 1, 0, 1), ("fp", 1, 7),
-    ("ag", 1, 0, 1, 1), ("ag", 1, 1, 1, 1), ("gz", 1), ("rx", 1, 4), ("rx", 1, 3), ("ag", 1, 0, 2, 1),
-    ("ag", 1, 1, 2, 1), ("rs", 1, 1, 1, 0), ("rs", 1, 0, 2, 0), ("rs", 1, 0, 1, 1), ("agc", 1, 1),
-    ("agc", 1, 6), ("ag", 1, 0, 0, 2), ("ag", 1, 1, 0, 2), ("agc", 1, 2), ("cr", 1, 5), ("fp", 1, 1),
-    ("ag", 1, 0, 1, 2), ("ag", 1, 1, 1, 2), ("fp", 1, 6), ("gb", 1), ("ag", 1, 0, 2, 2), ("ag", 1, 1, 2, 2),
-    ("rx", 1, 5), ("fp", 1, 2), ("rs", 1, 1, 0, 0), ("rs", 1, 0, 0, 1), ("rs", 1, 1, 2, 1), ("rs", 1, 0, 2, 1),
-    ("gs", 1), ("rs", 1, 1, 1, 1), ("agc", 1, 5), ("agc", 1, 3), ("cr", 1, 2), ("cr", 1, 6),
-    ("ag", 1, 0, 0, 3), ("ag", 1, 1, 2, 3), ("fp", 1, 5), ("ag", 1, 0, 1, 3), ("fp", 1, 3), ("rx", 1, 2),
-    ("rx", 1, 6), ("rs", 1, 1, 0, 1), ("rs", 1, 0, 1, 2), ("rs", 1, 1, 2, 2), ("gf", 1), ("rs", 1, 0, 2, 2),
-    ("rs", 1, 1, 1, 2), ("agc", 1, 4), ("cr", 1, 1), ("cr", 1, 7), ("rs", 1, 0, 0, 2), ("fp", 1, 4), ("fs", 1),
-    ("rx", 1, 1), ("rs", 1, 1, 0, 2), ("rs", 1, 0, 1, 3), ("cr", 1, 0), ("rx", 1, 7), ("rs", 1, 1, 2, 3),
-    ("rs", 1, 0, 2, 3), ("rs", 1, 1, 1, 3), ("rx", 1, 0), ("rs", 1, 0, 0, 3), ("rs", 1, 1, 0, 3), ("fsum", 1),
-    ("rp", 1), ("nl", 1), ("fw", 1),
+    ("ld",), ("gram", 0), ("cr", 0, 4), ("cr", 0, 3), ("cr", 0, 5), ("cr", 0, 2), ("cr", 0, 6), ("cr", 0, 1),
+    ("cr", 0, 7), ("cr", 0, 0), ("bar",), ("agb", 0), ("gms", 0), ("crs", 4), ("crs", 5), ("crs", 2),
+    ("crs", 1), ("crs", 3), ("crs", 6), ("crs", 0), ("crs", 7), ("gp", 0), ("rs", 0, 1, 1, 0), ("rx", 0, 4),
+    ("rs", 0, 0, 2, 0), ("agp", 0), ("rx", 0, 5), ("rs", 0, 1, 2, 1), ("ag", 0, 0, 0, 0), ("ag", 0, 1, 0, 0),
+    ("agc", 0, 0), ("gz", 0), ("rx", 0, 2), ("ag", 0, 0, 1, 0), ("ag", 0, 1, 1, 0), ("rx", 0, 1),
+    ("rs", 0, 1, 0, 0), ("rs", 0, 0, 1, 1), ("rx", 0, 3), ("rs", 0, 0, 2, 1), ("rs", 0, 1, 1, 1), ("rx", 0, 6),
+    ("ag", 0, 1, 2, 0), ("ag", 0, 0, 2, 0), ("agc", 0, 7), ("rx", 0, 0), ("rs", 0, 1, 2, 2),
+    ("ag", 0, 0, 0, 1), ("rx", 0, 7), ("agc", 0, 1), ("ag", 0, 1, 0, 1), ("fp", 0, 0), ("fp", 0, 7),
+    ("fp", 0, 1), ("rs", 0, 0, 1, 2), ("rs", 0, 0, 0, 1), ("gb", 0), ("ag", 0, 0, 1, 1), ("ag", 0, 1, 1, 1),
+    ("rs", 0, 1, 0, 1), ("rs", 0, 0, 2, 2), ("rs", 0, 1, 1, 2), ("ag", 0, 0, 2, 1), ("ag", 0, 1, 2, 1),
+    ("ag", 0, 0, 0, 2), ("agc", 0, 6), ("rs", 0, 1, 2, 3), ("rs", 0, 0, 1, 3), ("fp", 0, 6),
+    ("ag", 0, 1, 0, 2), ("rs", 0, 0, 0, 2), ("agc", 0, 2), ("gs", 0), ("ag", 0, 1, 1, 2), ("ag", 0, 0, 1, 2),
+    ("fp", 0, 2), ("gf", 0), ("agc", 0, 5), ("rs", 0, 1, 0, 2), ("rs", 0, 0, 2, 3), ("agc", 0, 3),
+    ("rs", 0, 1, 1, 3), ("ag", 0, 0, 2, 2), ("ag", 0, 1, 2, 2), ("ag", 0, 0, 0, 3), ("gy", 0), ("fp", 0, 5),
+    ("fp", 0, 3), ("rs", 0, 1, 0, 3), ("rs", 0, 0, 0, 3), ("agc", 0, 4), ("ag", 0, 0, 1, 3),
+    ("ag", 0, 1, 2, 3), ("rp", 0), ("fp", 0, 4), ("fs", 0), ("nl", 0), ("agb", 1), ("fx", 0), ("agp", 1),
+    ("ag", 1, 0, 0, 0), ("ag", 1, 1, 0, 0), ("agc", 1, 0), ("ag", 1, 0, 1, 0), ("ag", 1, 1, 1, 0), ("fsum", 0),
+    ("ag", 1, 0, 2, 0), ("ag", 1, 1, 2, 0), ("agc", 1, 7), ("ag", 1, 0, 0, 1), ("ag", 1, 1, 0, 1), ("fw", 0),
+    ("gram", 1), ("gms", 1), ("cr", 1, 4), ("agc", 1, 1), ("cr", 1, 3), ("ag", 1, 1, 1, 1), ("ag", 1, 0, 1, 1),
+    ("gp", 1), ("cr", 1, 5), ("cr", 1, 2), ("ag", 1, 0, 2, 1), ("rx", 1, 4), ("agc", 1, 6), ("ag", 1, 1, 2, 1),
+    ("cr", 1, 6), ("cr", 1, 1), ("ag", 1, 0, 0, 2), ("ag", 1, 1, 0, 2), ("rx", 1, 3), ("cr", 1, 7),
+    ("cr", 1, 0), ("gz", 1), ("ag", 1, 0, 1, 2), ("ag", 1, 1, 1, 2), ("agc", 1, 2), ("rx", 1, 5), ("fp", 1, 0),
+    ("ag", 1, 0, 2, 2), ("ag", 1, 1, 2, 2), ("rx", 1, 2), ("agc", 1, 5), ("rs", 1, 0, 2, 0), ("fp", 1, 7),
+    ("ag", 1, 0, 0, 3), ("agc", 1, 3), ("rx", 1, 6), ("rs", 1, 1, 0, 0), ("rs", 1, 0, 1, 1), ("fp", 1, 1),
+    ("gb", 1), ("rx", 1, 1), ("rs", 1, 0, 0, 1), ("rs", 1, 1, 2, 1), ("rs", 1, 1, 1, 0), ("fp", 1, 6),
+    ("ag", 1, 0, 1, 3), ("ag", 1, 1, 2, 3), ("rx", 1, 7), ("rx", 1, 0), ("rs", 1, 0, 2, 1), ("fp", 1, 2),
+    ("rs", 1, 1, 0, 1), ("fp", 1, 5), ("agc", 1, 4), ("rs", 1, 1, 2, 2), ("rs", 1, 0, 1, 2), ("fp", 1, 3),
+    ("rs", 1, 0, 0, 2), ("gs", 1), ("rs", 1, 1, 1, 1), ("fp", 1, 4), ("fs", 1), ("gf", 1), ("rs", 1, 0, 2, 2),
+    ("rs", 1, 1, 0, 2), ("rs", 1, 0, 1, 3), ("rs", 1, 1, 2, 3), ("rs", 1, 0, 0, 3), ("rs", 1, 1, 1, 2),
+    ("gy", 1), ("fx", 1), ("rs", 1, 0, 2, 3), ("rs", 1, 1, 0, 3), ("fsum", 1), ("rs", 1, 1, 1, 3), ("rp", 1),
+    ("nl", 1), ("fw", 1),
 )
 
 
@@ -63,7 +64,7 @@
     rate_z, rate_w,
     x_hbm, z_hbm, w_hbm, mask, modality_hbm, z_out, w_out,
     x, obs, zb, zt, zf, wf, wg, own, sib_out, sib_in, ring_out, ring_in, x_out, x_in, pair_out, pair_in,
-    g_local, g_sib, g_half, g_pair, g_z, g_all, pz, z_in_parts, z_new,
+    g_local, g_sib, g_half, g_pair, g_z, g_all, pz, z_in_parts, z_sum, z_new,
     z_in, w_in, w_new, modality, x_sem, in_sem, out_sem, ag_s, ag_r, agx_s, agx_r, ags_s, ags_r, rs_s, rs_r, rsa_s, rsa_r, rsx_s, rsx_r, rss_s, rss_r,
     g_s, g_r, gz_s, gz_r, gf_s, gf_r, az_s, az_r, an_s, an_r,
 ):
@@ -73,14 +74,18 @@
     xh = (s // 2) % 2
     c = s % 2
     batch = z // 4
+    xl = k // 4
+    y = k % 4
     sibling = {"sample": z * 4 + xh * 2 + (1 - c)}
     partner = {"sample": z * 4 + (1 - xh) * 2 + c}
 
     def along(step):
         return {"sample": ((z + step + NZ) % NZ) * 4 + xh * 2 + c}
 
-    def peer(off):
-        return {"feat": (k + off) % NF}
+    def y_peer(off):
+        return {"feat": xl * 4 + (y + off) % 4}
+
+    x_peer = {"feat": (1 - xl) * 4 + y}
 
     neighbour = (along(1), along(-1))
     started = []
@@ -110,7 +115,7 @@
     load_x.start()
 
     barrier = pltpu.get_barrier_semaphore()
-    greet = [sibling, partner] + [along(d) for d in range(1, NZ)] + [peer(d) for d in range(1, NF)]
+    greet = [sibling, partner] + [along(d) for d in range(1, NZ)] + [y_peer(d) for d in (1, 2, 3)] + [x_peer]
     for device in greet:
         pl.semaphore_signal(barrier, inc=1, device_id=device, device_id_type=pl.DeviceIdType.MESH)
     loads[0].wait()
@@ -118,7 +123,6 @@
     loads[1].wait()
     zb[0] = z_in[...].astype(BF)
     loads[2].wait()
-    pl.semaphore_wait(barrier, len(greet))
 
     waited = set()
 
@@ -220,13 +224,21 @@
                     own[slot] = value
                 else:
                     sib_out[it, slot] = value.astype(BF)
-                    sem = it * 2 * NZ + slot
-                    copy(
-                        sib_out.at[it, slot], sib_in.at[it, slot], rss_s.at[sem], rss_r.at[sem], sibling
-                    ).start()
+                    if it == 1:
+                        sem = it * 2 * NZ + slot
+                        copy(
+                            sib_out.at[it, slot], sib_in.at[it, slot], rss_s.at[sem], rss_r.at[sem], sibling
+                        ).start()
             return carry
 
         lax.fori_loop(0, 2, body, 0)
+
+    def cross_send(rel):
+        for col in (0, 1):
+            slot = rel * 2 + col
+            copy(
+                sib_out.at[0, slot], sib_in.at[0, slot], rss_s.at[slot], rss_r.at[slot], sibling
+            ).start()
 
     def cross_end(it):
         def body(slot, carry):
@@ -283,15 +295,20 @@
         copy(pair_out.at[it], pair_in.at[it], rsx_s.at[it], rsx_r.at[it], partner).wait_recv()
         return jnp.concatenate([low, high + pair_in[it].astype(F32)], axis=0)
 
-    half = pl.multiple_of(k * 32 + c * 16, 16)
-    other_half = pl.multiple_of(k * 32 + (1 - c) * 16, 16)
-    base = pl.multiple_of(k * 32 + c * 16 + xh * 8, 8)
+    rows64 = pl.multiple_of(y * 64, 64)
+
+    kk = y * 2 + xl
+    half = pl.multiple_of(kk * 32 + c * 16, 16)
+    other_half = pl.multiple_of(kk * 32 + (1 - c) * 16, 16)
+    base = pl.multiple_of(kk * 32 + c * 16 + xh * 8, 8)
     mine8 = pl.multiple_of(xh * 8, 8)
     other8 = pl.multiple_of((1 - xh) * 8, 8)
 
     def gram(it):
         zt[...] = zb[it].astype(F32).T.astype(BF)
         g_local[it] = nn(zt[...], zb[it])
+
+    def gram_send(it):
         i = it * 4
         send(g_local.at[it, pl.ds(other_half, 16)], g_sib.at[it], g_s.at[i], g_r.at[i], sibling)
 
@@ -323,7 +340,7 @@
         send(block, block, g_s.at[it * 4 + 2], g_r.at[it * 4 + 2], partner)
 
     def gram_sibling(it):
-        rows = pl.multiple_of(k * 32 + c * 16 + (1 - xh) * 8, 8)
+        rows = pl.multiple_of(kk * 32 + c * 16 + (1 - xh) * 8, 8)
         block = g_all.at[it, :, pl.ds(rows, 8)]
         copy(block, block, g_s.at[it * 4 + 2], g_r.at[it * 4 + 2], partner).wait_recv()
         block = g_all.at[it, :, pl.ds(half, 16)]
@@ -332,17 +349,22 @@
     def gram_feat(it):
         block = g_all.at[it, :, pl.ds(other_half, 16)]
         copy(block, block, g_s.at[it * 4 + 3], g_r.at[it * 4 + 3], sibling).wait_recv()
-        block = g_all.at[it, :, pl.ds(pl.multiple_of(k * 32, 32), 32)]
-        for off in range(1, NF):
-            i = it * NF + off
-            send(block, block, gf_s.at[i], gf_r.at[i], peer(off))
+        block = g_all.at[it, :, pl.ds(pl.multiple_of(kk * 32, 32), 32)]
+        send(block, block, gf_s.at[it * 4], gf_r.at[it * 4], x_peer)
+
+    def gram_y(it):
+        block = g_all.at[it, :, pl.ds(pl.multiple_of(y * 64 + (1 - xl) * 32, 32), 32)]
+        copy(block, block, gf_s.at[it * 4], gf_r.at[it * 4], x_peer).wait_recv()
+        block = g_all.at[it, :, pl.ds(rows64, 64)]
+        for off in (1, 2, 3):
+            i = it * 4 + off
+            send(block, block, gf_s.at[i], gf_r.at[i], y_peer(off))
 
     def new_loadings(it):
-        for off in range(1, NF):
-            i = it * NF + off
-            rows = pl.multiple_of(((k + NF - off) % NF) * 32, 32)
-            block = g_all.at[it, :, pl.ds(rows, 32)]
-            copy(block, block, gf_s.at[i], gf_r.at[i], peer(off)).wait_recv()
+        for off in (1, 2, 3):
+            i = it * 4 + off
+            block = g_all.at[it, :, pl.ds(pl.multiple_of(((y + 4 - off) % 4) * 64, 64), 64)]
+            copy(block, block, gf_s.at[i], gf_r.at[i], y_peer(off)).wait_recv()
         cols = pl.ds(pl.multiple_of(s * T, T), T)
         w = wg[it, s]
         grad = jnp.zeros((T, T), F32)
@@ -360,42 +382,48 @@
             w_new[...] = new
             pltpu.make_async_copy(w_new, w_out, out_sem.at[0]).start()
 
-    rows32 = pl.multiple_of(k * 32, 32)
-
     def factors_send(it):
-        for off in range(1, NF):
-            i = it * NF + off
-            rows = pl.multiple_of(((k + off) % NF) * 32, 32)
-            send(pz.at[it, pl.ds(rows, 32)], z_in_parts.at[it, off], az_s.at[i], az_r.at[i], peer(off))
+        for off in (1, 2, 3):
+            i = it * 4 + off
+            there = pl.multiple_of(((y + off) % 4) * 64, 64)
+            send(pz.at[it, pl.ds(there, 64)], z_in_parts.at[it, off], az_s.at[i], az_r.at[i], y_peer(off))
+
+    def factors_across(it):
+        total = pz[it, pl.ds(rows64, 64)]
+        for off in (1, 2, 3):
+            i = it * 4 + off
+            slot = z_in_parts.at[it, off]
+            copy(slot, slot, az_s.at[i], az_r.at[i], y_peer(off)).wait_recv()
+            total = total + z_in_parts[it, off]
+        z_sum[it, 0] = total
+        send(z_sum.at[it, 0], z_sum.at[it, 1], az_s.at[it * 4], az_r.at[it * 4], x_peer)
 
     def factors_sum(it):
-        total = pz[it, pl.ds(rows32, 32)]
-        for off in range(1, NF):
-            i = it * NF + off
-            slot = z_in_parts.at[it, off]
-            copy(slot, slot, az_s.at[i], az_r.at[i], peer(off)).wait_recv()
-            total = total + z_in_parts[it, off]
-        old = z_in[pl.ds(rows32, 32)] if it == 0 else zf[...]
-        new = old - rate_z * total
+        copy(z_sum.at[it, 0], z_sum.at[it, 1], az_s.at[it * 4], az_r.at[it * 4], x_peer).wait_recv()
+        old = z_in[pl.ds(rows64, 64)] if it == 0 else zf[...]
+        new = old - rate_z * (z_sum[it, 0] + z_sum[it, 1])
         if it == 0:
             zf[...] = new
-            zb[1, pl.ds(rows32, 32)] = new.astype(BF)
+            zb[1, pl.ds(rows64, 64)] = new.astype(BF)
         else:
-            z_new[pl.ds(rows32, 32)] = new
+            z_new[pl.ds(rows64, 64)] = new
         target = zb.at[1] if it == 0 else z_new
-        block = target.at[pl.ds(rows32, 32)]
-        for off in range(1, NF):
-            i = it * NF + off
-            send(block, block, an_s.at[i], an_r.at[i], peer(off))
+        block = target.at[pl.ds(rows64, 64)]
+        for off in (1, 2, 3):
+            i = it * 4 + off
+            send(block, block, an_s.at[i], an_r.at[i], y_peer(off))
 
     def factors_wait(it):
         target = zb.at[1] if it == 0 else z_new
-        for off in range(1, NF):
-            i = it * NF + off
-            block = target.at[pl.ds(pl.multiple_of(((k + NF - off) % NF) * 32, 32), 32)]
-            copy(block, block, an_s.at[i], an_r.at[i], peer(off)).wait_recv()
+        for off in (1, 2, 3):
+            i = it * 4 + off
+            block = target.at[pl.ds(pl.multiple_of(((y + 4 - off) % 4) * 64, 64), 64)]
+            copy(block, block, an_s.at[i], an_r.at[i], y_peer(off)).wait_recv()
         if it == 1:
             pltpu.make_async_copy(z_new, z_out, out_sem.at[1]).start()
+
+    def enter():
+        pl.semaphore_wait(barrier, len(greet))
 
     def load():
         for b in (0, 1):
@@ -410,6 +438,7 @@
         "fs": factors_send, "fsum": factors_sum, "fw": factors_wait,
         "gram": gram, "gp": gram_pair, "gz": gram_z, "gb": gram_batches, "gs": gram_sibling, "gf": gram_feat,
         "cr": cross, "rx": rs_across, "rs": rs_one, "rp": rs_pair_send, "nl": new_loadings, "ld": load,
+        "bar": enter, "crs": cross_send, "gms": gram_send, "gy": gram_y, "fx": factors_across,
     }
     for name, *where in ORDER:
         do[name](*where)
@@ -455,7 +484,7 @@
             pltpu.VMEM((2, 1, width), F32),
             pltpu.VMEM((ITERS, T, T), BF),
             pltpu.VMEM((T, T), BF),
-            pltpu.VMEM((32, T), F32),
+            pltpu.VMEM((64, T), F32),
             pltpu.VMEM((T, T), F32),
             pltpu.VMEM((ITERS, 32, T, T), BF),
             pltpu.VMEM((2 * NZ, T, T), F32),
@@ -474,7 +503,8 @@
             pltpu.VMEM((ITERS, NZ, 8, T), F32),
             pltpu.VMEM((ITERS, 2, T, T), F32),
             pltpu.VMEM((ITERS, T, T), F32),
-            pltpu.VMEM((ITERS, NF, 32, T), F32),
+            pltpu.VMEM((ITERS, 4, 64, T), F32),
+            pltpu.VMEM((ITERS, 2, 64, T), F32),
             pltpu.VMEM((T, T), F32),
             pltpu.VMEM((T, T), F32),
             pltpu.VMEM((T, T), F32),
@@ -491,9 +521,9 @@
             dma(ITERS * 16), dma(ITERS * 16),
             dma(ITERS * 4), dma(ITERS * 4),
             dma(ITERS * NZ), dma(ITERS * NZ),
-            dma(ITERS * NF), dma(ITERS * NF),
-            dma(ITERS * NF), dma(ITERS * NF),
-            dma(ITERS * NF), dma(ITERS * NF),
+            dma(ITERS * 4), dma(ITERS * 4),
+            dma(ITERS * 4), dma(ITERS * 4),
+            dma(ITERS * 4), dma(ITERS * 4),
         ],
         compiler_params=pltpu.CompilerParams(
             collective_id=0, has_side_effects=True, vmem_limit_bytes=60 * 1024 * 1024

time: 111 us -> 104 us (0.937); the launches traced: 110 us -> 104 us
  Pallas kernels: 109 us -> 103 us
    pallas_call x1, Pallas kernels: 107 us -> 102 us  [per_device(): pl.pallas_call(body, out_shape=(out, out), in_specs=[hbm, hbm, hbm, pl.Bl...]
where the time goes in v3:
time: 104 us
  Pallas kernels  103 us (99%)
    pallas_call x1, Pallas kernels, per_device(): pl.pallas_call(body, out_shape=(out, out), in_specs=[hbm, hbm, hbm, pl.Bl...  102 us

profile of v3, /device:TPU:2, one launch (start us, length us, event | category | flops | bytes accessed | tf_op | source)
XLA Modules:
  0.0 104.1 jit_solution(9940051912465595216)
XLA Ops:
  0.6 101.7 %shard_map.68 = (f32[256,256]{1,0:T(8,128)}, f32[256,256]{1,0:T(8,128)}) custom-call(bf16[256,8192]{1,0:T(8,128)(2,1)} %refs_0_.1, f32[256,256]{1,0:T(8,128)} %refs_1_.1, f32[256,256]{1,0:T(8,128)} %refs_2_.1, s32[2,5]{1,0:T(2,128)} %refs_3_.1, s32[1,8192]{1,0:T(1,128)} %bitcast.1), custom_call_target="tpu_custom_call" | custom-call | tf_op jit(solution)/shard_map/pallas_call | solution.py:475
  102.3 1.8 %shard_map.69 = (f32[256,256]{1,0:T(8,128)}, f32[256,256]{1,0:T(8,128)}) custom-call(f32[256,256]{1,0:T(8,128)} %get-tuple-element.4.z_from, f32[256,256]{1,0:T(8,128)} %get-tuple-element.5.w_from), custom_call_target="tpu_custom_call" | custom-call | tf_op jit(solution)/shard_map/pallas_call | solution.py:532

commit v4 on v3

--- a/solution.py
+++ b/solution.py
@@ -18,37 +18,39 @@
 AG_FULL = ((0, 0), (0, 1), (1, 2))
 RS_FULL = ((1, 0), (1, 1), (0, 2))
 ORDER = (
-    ("ld",), ("gram", 0), ("cr", 0, 4), ("cr", 0, 3), ("cr", 0, 5), ("cr", 0, 2), ("cr", 0, 6), ("cr", 0, 1),
-    ("cr", 0, 7), ("cr", 0, 0), ("bar",), ("agb", 0), ("gms", 0), ("crs", 4), ("crs", 5), ("crs", 2),
-    ("crs", 1), ("crs", 3), ("crs", 6), ("crs", 0), ("crs", 7), ("gp", 0), ("rs", 0, 1, 1, 0), ("rx", 0, 4),
-    ("rs", 0, 0, 2, 0), ("agp", 0), ("rx", 0, 5), ("rs", 0, 1, 2, 1), ("ag", 0, 0, 0, 0), ("ag", 0, 1, 0, 0),
-    ("agc", 0, 0), ("gz", 0), ("rx", 0, 2), ("ag", 0, 0, 1, 0), ("ag", 0, 1, 1, 0), ("rx", 0, 1),
-    ("rs", 0, 1, 0, 0), ("rs", 0, 0, 1, 1), ("rx", 0, 3), ("rs", 0, 0, 2, 1), ("rs", 0, 1, 1, 1), ("rx", 0, 6),
-    ("ag", 0, 1, 2, 0), ("ag", 0, 0, 2, 0), ("agc", 0, 7), ("rx", 0, 0), ("rs", 0, 1, 2, 2),
-    ("ag", 0, 0, 0, 1), ("rx", 0, 7), ("agc", 0, 1), ("ag", 0, 1, 0, 1), ("fp", 0, 0), ("fp", 0, 7),
-    ("fp", 0, 1), ("rs", 0, 0, 1, 2), ("rs", 0, 0, 0, 1), ("gb", 0), ("ag", 0, 0, 1, 1), ("ag", 0, 1, 1, 1),
-    ("rs", 0, 1, 0, 1), ("rs", 0, 0, 2, 2), ("rs", 0, 1, 1, 2), ("ag", 0, 0, 2, 1), ("ag", 0, 1, 2, 1),
-    ("ag", 0, 0, 0, 2), ("agc", 0, 6), ("rs", 0, 1, 2, 3), ("rs", 0, 0, 1, 3), ("fp", 0, 6),
-    ("ag", 0, 1, 0, 2), ("rs", 0, 0, 0, 2), ("agc", 0, 2), ("gs", 0), ("ag", 0, 1, 1, 2), ("ag", 0, 0, 1, 2),
-    ("fp", 0, 2), ("gf", 0), ("agc", 0, 5), ("rs", 0, 1, 0, 2), ("rs", 0, 0, 2, 3), ("agc", 0, 3),
-    ("rs", 0, 1, 1, 3), ("ag", 0, 0, 2, 2), ("ag", 0, 1, 2, 2), ("ag", 0, 0, 0, 3), ("gy", 0), ("fp", 0, 5),
-    ("fp", 0, 3), ("rs", 0, 1, 0, 3), ("rs", 0, 0, 0, 3), ("agc", 0, 4), ("ag", 0, 0, 1, 3),
-    ("ag", 0, 1, 2, 3), ("rp", 0), ("fp", 0, 4), ("fs", 0), ("nl", 0), ("agb", 1), ("fx", 0), ("agp", 1),
-    ("ag", 1, 0, 0, 0), ("ag", 1, 1, 0, 0), ("agc", 1, 0), ("ag", 1, 0, 1, 0), ("ag", 1, 1, 1, 0), ("fsum", 0),
-    ("ag", 1, 0, 2, 0), ("ag", 1, 1, 2, 0), ("agc", 1, 7), ("ag", 1, 0, 0, 1), ("ag", 1, 1, 0, 1), ("fw", 0),
-    ("gram", 1), ("gms", 1), ("cr", 1, 4), ("agc", 1, 1), ("cr", 1, 3), ("ag", 1, 1, 1, 1), ("ag", 1, 0, 1, 1),
-    ("gp", 1), ("cr", 1, 5), ("cr", 1, 2), ("ag", 1, 0, 2, 1), ("rx", 1, 4), ("agc", 1, 6), ("ag", 1, 1, 2, 1),
-    ("cr", 1, 6), ("cr", 1, 1), ("ag", 1, 0, 0, 2), ("ag", 1, 1, 0, 2), ("rx", 1, 3), ("cr", 1, 7),
-    ("cr", 1, 0), ("gz", 1), ("ag", 1, 0, 1, 2), ("ag", 1, 1, 1, 2), ("agc", 1, 2), ("rx", 1, 5), ("fp", 1, 0),
-    ("ag", 1, 0, 2, 2), ("ag", 1, 1, 2, 2), ("rx", 1, 2), ("agc", 1, 5), ("rs", 1, 0, 2, 0), ("fp", 1, 7),
-    ("ag", 1, 0, 0, 3), ("agc", 1, 3), ("rx", 1, 6), ("rs", 1, 1, 0, 0), ("rs", 1, 0, 1, 1), ("fp", 1, 1),
-    ("gb", 1), ("rx", 1, 1), ("rs", 1, 0, 0, 1), ("rs", 1, 1, 2, 1), ("rs", 1, 1, 1, 0), ("fp", 1, 6),
-    ("ag", 1, 0, 1, 3), ("ag", 1, 1, 2, 3), ("rx", 1, 7), ("rx", 1, 0), ("rs", 1, 0, 2, 1), ("fp", 1, 2),
-    ("rs", 1, 1, 0, 1), ("fp", 1, 5), ("agc", 1, 4), ("rs", 1, 1, 2, 2), ("rs", 1, 0, 1, 2), ("fp", 1, 3),
-    ("rs", 1, 0, 0, 2), ("gs", 1), ("rs", 1, 1, 1, 1), ("fp", 1, 4), ("fs", 1), ("gf", 1), ("rs", 1, 0, 2, 2),
-    ("rs", 1, 1, 0, 2), ("rs", 1, 0, 1, 3), ("rs", 1, 1, 2, 3), ("rs", 1, 0, 0, 3), ("rs", 1, 1, 1, 2),
-    ("gy", 1), ("fx", 1), ("rs", 1, 0, 2, 3), ("rs", 1, 1, 0, 3), ("fsum", 1), ("rs", 1, 1, 1, 3), ("rp", 1),
-    ("nl", 1), ("fw", 1),
+    ("ld",), ("gram", 0), ("cr", 0, 4), ("cr", 0, 3), ("cr", 0, 5), ("cr", 0, 2), ("bar",), ("agb", 0),
+    ("cr", 0, 6), ("cr", 0, 1), ("cr", 0, 7), ("gms", 0), ("crs", 4), ("cr", 0, 0), ("crs", 5), ("crs", 0),
+    ("crs", 3), ("crs", 1), ("crs", 6), ("crs", 7), ("gp", 0), ("crs", 2), ("rs", 0, 1, 1, 0), ("agp", 0),
+    ("rx", 0, 4), ("rs", 0, 0, 2, 0), ("ag", 0, 0, 0, 0), ("ag", 0, 1, 0, 0), ("rx", 0, 5), ("gz", 0),
+    ("rs", 0, 1, 2, 1), ("agc", 0, 0), ("ag", 0, 0, 1, 0), ("rx", 0, 0), ("ag", 0, 1, 1, 0),
+    ("rs", 0, 0, 1, 1), ("rx", 0, 3), ("rs", 0, 1, 0, 0), ("rs", 0, 1, 1, 1), ("ag", 0, 0, 2, 0), ("rx", 0, 1),
+    ("agc", 0, 7), ("ag", 0, 1, 2, 0), ("rx", 0, 6), ("rs", 0, 0, 2, 1), ("agc", 0, 1), ("rx", 0, 7),
+    ("ag", 0, 1, 0, 1), ("ag", 0, 0, 0, 1), ("rx", 0, 2), ("gb", 0), ("fp", 0, 0), ("fq", 0, 0),
+    ("rs", 0, 1, 2, 2), ("fp", 0, 7), ("ag", 0, 0, 1, 1), ("fp", 0, 1), ("rs", 0, 0, 0, 1), ("fq", 0, 1),
+    ("rs", 0, 0, 1, 2), ("fq", 0, 7), ("ag", 0, 1, 1, 1), ("rs", 0, 1, 0, 1), ("ag", 0, 0, 2, 1),
+    ("rs", 0, 1, 1, 2), ("rs", 0, 0, 2, 2), ("ag", 0, 1, 2, 1), ("ag", 0, 0, 0, 2), ("agc", 0, 2),
+    ("ag", 0, 1, 0, 2), ("ag", 0, 0, 1, 2), ("fp", 0, 2), ("agc", 0, 6), ("fq", 0, 2), ("rs", 0, 1, 2, 3),
+    ("rs", 0, 0, 0, 2), ("gs", 0), ("fp", 0, 6), ("rs", 0, 0, 1, 3), ("ag", 0, 1, 1, 2), ("fq", 0, 6),
+    ("gf", 0), ("agc", 0, 5), ("rs", 0, 1, 0, 2), ("ag", 0, 0, 2, 2), ("agc", 0, 3), ("rs", 0, 1, 1, 3),
+    ("fp", 0, 5), ("rs", 0, 0, 2, 3), ("fq", 0, 5), ("ag", 0, 1, 2, 2), ("gy", 0), ("ag", 0, 0, 0, 3),
+    ("fp", 0, 3), ("fq", 0, 3), ("ag", 0, 0, 1, 3), ("rs", 0, 1, 0, 3), ("rs", 0, 0, 0, 3), ("agc", 0, 4),
+    ("ag", 0, 1, 2, 3), ("rp", 0), ("fp", 0, 4), ("fq", 0, 4), ("fs", 0), ("nl", 0), ("agb", 1), ("fx", 0),
+    ("agp", 1), ("ag", 1, 0, 0, 0), ("ag", 1, 1, 0, 0), ("agc", 1, 0), ("ag", 1, 0, 1, 0), ("ag", 1, 1, 1, 0),
+    ("fsum", 0), ("ag", 1, 0, 2, 0), ("ag", 1, 1, 2, 0), ("agc", 1, 7), ("ag", 1, 0, 0, 1), ("ag", 1, 1, 0, 1),
+    ("agc", 1, 1), ("fw", 0), ("gram", 1), ("ag", 1, 1, 1, 1), ("gms", 1), ("ag", 1, 0, 1, 1), ("fp", 1, 0),
+    ("fq", 1, 0), ("fp", 1, 7), ("ag", 1, 0, 2, 1), ("gp", 1), ("agc", 1, 6), ("ag", 1, 1, 2, 1), ("fq", 1, 7),
+    ("cr", 1, 4), ("ag", 1, 0, 0, 2), ("ag", 1, 1, 0, 2), ("agc", 1, 2), ("cr", 1, 3), ("gz", 1), ("fp", 1, 6),
+    ("fq", 1, 6), ("rs", 1, 0, 2, 0), ("rx", 1, 4), ("rs", 1, 1, 1, 0), ("cr", 1, 5), ("ag", 1, 0, 2, 2),
+    ("cr", 1, 2), ("ag", 1, 1, 2, 2), ("agc", 1, 5), ("ag", 1, 1, 1, 2), ("rs", 1, 0, 1, 1), ("rx", 1, 3),
+    ("fp", 1, 1), ("ag", 1, 0, 0, 3), ("agc", 1, 3), ("ag", 1, 0, 1, 2), ("fp", 1, 2), ("rs", 1, 1, 2, 1),
+    ("fq", 1, 2), ("gb", 1), ("rs", 1, 1, 0, 0), ("rx", 1, 5), ("rx", 1, 2), ("cr", 1, 6), ("cr", 1, 1),
+    ("rs", 1, 0, 0, 1), ("rs", 1, 0, 2, 1), ("fp", 1, 3), ("fp", 1, 5), ("rs", 1, 0, 1, 2), ("ag", 1, 1, 2, 3),
+    ("agc", 1, 4), ("fq", 1, 3), ("rx", 1, 6), ("gs", 1), ("fq", 1, 5), ("rs", 1, 1, 2, 2), ("ag", 1, 0, 1, 3),
+    ("rx", 1, 1), ("fq", 1, 1), ("gf", 1), ("cr", 1, 7), ("rs", 1, 1, 0, 1), ("cr", 1, 0), ("rs", 1, 0, 0, 2),
+    ("fp", 1, 4), ("fq", 1, 4), ("fs", 1), ("rs", 1, 1, 1, 1), ("rs", 1, 0, 2, 2), ("rx", 1, 7),
+    ("rs", 1, 1, 2, 3), ("rx", 1, 0), ("rs", 1, 0, 1, 3), ("rs", 1, 1, 0, 2), ("gy", 1), ("rs", 1, 0, 0, 3),
+    ("rs", 1, 1, 1, 2), ("rs", 1, 0, 2, 3), ("fx", 1), ("rs", 1, 1, 0, 3), ("fsum", 1), ("rs", 1, 1, 1, 3),
+    ("rp", 1), ("nl", 1), ("fw", 1),
 )
 
 
@@ -192,23 +194,25 @@
             i = ((it * NZ + rel % NZ) * 2 + col) * 2 + h
             copy(block, block, ags_s.at[i], ags_r.at[i], sibling).wait_recv()
 
+    def factor_half(it, rel, j):
+        there = (z + rel + NZ) % NZ
+        w = wg[it, pl.ds(there * 4 + j * 2, 2)].reshape(2 * T, T)
+        cols = pl.ds(pl.multiple_of(there * 4 * T + j * 2 * T, 2 * T), 2 * T)
+        pred = nt(zb[it], w)
+        resid = (obs[batch, :, cols] * (pred - x[:, cols].astype(F32))).astype(BF)
+        part = nn(resid, w)
+        if ("pz", it) in waited:
+            pz[it] += part
+        else:
+            pz[it] = part
+        waited.add(("pz", it))
+
     def factor_part(it, rel):
         ag_from_sibling(it, rel)
-        first = ("pz", it) not in waited
-        waited.add(("pz", it))
-        there = (z + rel + NZ) % NZ
-
-        def body(j, carry):
-            w = wg[it, pl.ds(there * 4 + j * 2, 2)].reshape(2 * T, T)
-            cols = pl.ds(pl.multiple_of(there * 4 * T + j * 2 * T, 2 * T), 2 * T)
-            pred = nt(zb[it], w)
-            resid = (obs[batch, :, cols] * (pred - x[:, cols].astype(F32))).astype(BF)
-            pz[it] += nn(resid, w)
-            return carry
-
-        if first:
-            pz[it] = jnp.zeros((T, T), F32)
-        lax.fori_loop(0, 2, body, 0)
+        factor_half(it, rel, 0)
+
+    def factor_rest(it, rel):
+        factor_half(it, rel, 1)
 
     def cross(it, rel):
         there = (z + rel) % NZ
@@ -434,19 +438,26 @@
         load_x.wait()
 
     do = {
-        "agb": ag_begin, "agp": ag_pair, "ag": ag_one, "agc": ag_crossed, "fp": factor_part,
+        "agb": ag_begin, "agp": ag_pair, "ag": ag_one, "agc": ag_crossed, "fp": factor_part, "fq": factor_rest,
         "fs": factors_send, "fsum": factors_sum, "fw": factors_wait,
         "gram": gram, "gp": gram_pair, "gz": gram_z, "gb": gram_batches, "gs": gram_sibling, "gf": gram_feat,
         "cr": cross, "rx": rs_across, "rs": rs_one, "rp": rs_pair_send, "nl": new_loadings, "ld": load,
         "bar": enter, "crs": cross_send, "gms": gram_send, "gy": gram_y, "fx": factors_across,
     }
-    for name, *where in ORDER:
+    marks = []
+    ended = 0
+    for step, (name, *where) in enumerate(ORDER):
         do[name](*where)
-
-    for one in started:
+        marks.append(len(started))
+        if step >= 40:
+            for one in started[ended:marks[step - 40]]:
+                one.wait_send()
+            ended = marks[step - 40]
+        if (name, where) == ("agb", [1]):
+            cross_end(0)
+    for one in started[ended:]:
         one.wait_send()
-    for it in range(ITERS):
-        cross_end(it)
+    cross_end(1)
     pltpu.make_async_copy(w_new, w_out, out_sem.at[0]).wait()
     pltpu.make_async_copy(z_new, z_out, out_sem.at[1]).wait()
 

time: 104 us -> 102 us (0.981)
  Pallas kernels: 103 us -> 101 us
    pallas_call x1, Pallas kernels: 102 us -> 99.2 us  [per_device(): pl.pallas_call(body, out_shape=(out, out), in_specs=[hbm, hbm, hbm, pl.Bl...]
where the time goes in v4:
time: 102 us
  Pallas kernels  101 us (99%)
    pallas_call x1, Pallas kernels, per_device(): pl.pallas_call(body, out_shape=(out, out), in_specs=[hbm, hbm, hbm, pl.Bl...  99.2 us

profile of v4, /device:TPU:2, one launch (start us, length us, event | category | flops | bytes accessed | tf_op | source)
XLA Modules:
  0.0 101.7 jit_solution(11326652278842548660)
XLA Ops:
  0.6 99.2 %shard_map.68 = (f32[256,256]{1,0:T(8,128)}, f32[256,256]{1,0:T(8,128)}) custom-call(bf16[256,8192]{1,0:T(8,128)(2,1)} %refs_0_.1, f32[256,256]{1,0:T(8,128)} %refs_1_.1, f32[256,256]{1,0:T(8,128)} %refs_2_.1, s32[2,5]{1,0:T(2,128)} %refs_3_.1, s32[1,8192]{1,0:T(1,128)} %bitcast.1), custom_call_target="tpu_custom_call" | custom-call | tf_op jit(solution)/shard_map/pallas_call | solution.py:486
  99.8 1.8 %shard_map.69 = (f32[256,256]{1,0:T(8,128)}, f32[256,256]{1,0:T(8,128)}) custom-call(f32[256,256]{1,0:T(8,128)} %get-tuple-element.4.z_from, f32[256,256]{1,0:T(8,128)} %get-tuple-element.5.w_from), custom_call_target="tpu_custom_call" | custom-call | tf_op jit(solution)/shard_map/pallas_call | solution.py:543
